TPU v7x, 32 devices: a whole 2x2x4 slice. The times are simulated.
32 devices in a mesh: batch: 4 (over z), wide: 8 (over y, x, core).
Axes of the slice: x: 2, y: 2, z: 4, core: 2. Of those that a mesh axis runs over, the one named last changes fastest.
Arguments:
- tokens: bfloat16 [2048, 8, 1024], P('wide', 'batch'), may hold values from -6 to 6
- lengths: int32 [8, 16], P('batch'), may hold values from 0 to 2048, as said below
- cotangent: bfloat16 [2048, 8, 1024], P('wide', 'batch'), may hold values from -6 to 6
- first_gain: float32 [1024], replicated, may hold values from 0.25 to 1.75
- query_heads: bfloat16 [1024, 96], replicated, may hold values from -0.4375 to 0.4375
- query_basis: bfloat16 [1024, 384], replicated, may hold values from -0.1875 to 0.1875
- key_heads: bfloat16 [1024, 32], replicated, may hold values from -0.4375 to 0.4375
- key_basis: bfloat16 [1024, 128], replicated, may hold values from -0.1875 to 0.1875
- value_heads: bfloat16 [1024, 32], replicated, may hold values from -0.1875 to 0.1875
- value_basis: bfloat16 [1024, 128], replicated, may hold values from -0.1875 to 0.1875
- output_weight: bfloat16 [1024, 1024], replicated, may hold values from -0.75 to 0.75
- second_gain: float32 [1024], replicated, may hold values from 0.25 to 1.75
- gate_weight: bfloat16 [1024, 2816], P(None, 'wide'), may hold values from -0.1875 to 0.1875
- up_weight: bfloat16 [1024, 2816], P(None, 'wide'), may hold values from -0.1875 to 0.1875
- down_projection_weight: bfloat16 [2816, 1024], P('wide'), may hold values from -0.109375 to 0.109375
Outputs:
- output: bfloat16 [2048, 8, 1024], P('wide', 'batch')
- tokens_gradient: float32 [2048, 8, 1024], P('wide', 'batch')
- first_gain_gradient: float32 [1024], P('wide')
- query_heads_gradient: float32 [1024, 96], P('wide')
- query_basis_gradient: float32 [1024, 384], P('wide')
- key_heads_gradient: float32 [1024, 32], P('wide')
- key_basis_gradient: float32 [1024, 128], P('wide')
- value_heads_gradient: float32 [1024, 32], P('wide')
- value_basis_gradient: float32 [1024, 128], P('wide')
- output_weight_gradient: float32 [1024, 1024], P('wide')
- second_gain_gradient: float32 [1024], P('wide')
- gate_weight_gradient: float32 [1024, 2816], P(None, 'wide')
- up_weight_gradient: float32 [1024, 2816], P(None, 'wide')
- down_weight_gradient: float32 [2816, 1024], P('wide')
Inputs may be any that keep to these rules, and one draw needn't show every extreme that they name: In each packed row the nonzero lengths come first, each is 128 or more, and they sum to at most 2048; later slots hold 0, and the places after the last sequence are padding.
All inputs are finite; a program needn't handle non-finite values.
Results may differ from a plain program's by a relative error of at most 0.022.
The roundings to bfloat16 on the way count: a program that leaves them out, or rounds other values in their place, can miss the bound.
Values may be sent and summed in bfloat16 or wider, within the bound.
No kernel may reach another device: no remote copies, remote signals or barrier semaphores. Data moves between devices by JAX's collectives and lax.ppermute only.
A program may use at most 256 MiB of HBM per device.

v0:
```python
import jax
import jax.numpy as jnp
from jax import lax
from jax.sharding import PartitionSpec as P

HEADS = 16
HEAD_DIM = 64
Q_RANK = 6
KV_RANK = 2


highest = lax.Precision.HIGHEST
masked_score = -1e30


def rms_scale(values):
    return lax.rsqrt(jnp.mean(values * values, axis=-1, keepdims=True) + 1e-06)


def norm_backward(values, gain, scaled, upstream):
    weighted = upstream * gain
    inner = jnp.mean(values * weighted, axis=-1, keepdims=True)
    return scaled * weighted - values * (scaled * scaled * scaled) * inner


def rotate(values, cosine, sine):
    half = values.shape[-1] // 2
    first = values[..., :half]
    second = values[..., half:]
    return jnp.concatenate(
        [first * cosine - second * sine, first * sine + second * cosine], axis=-1
    )


def row_layout(lengths_row, places):
    ends = jnp.cumsum(lengths_row)
    passed = ends[None, :] <= places[:, None]
    segment = jnp.sum(passed.astype(jnp.int32), axis=1)
    start = jnp.max(jnp.where(passed, ends[None, :], 0), axis=1)
    valid = places < ends[-1]
    return (segment, places - start, valid)


def rope_tables(position):
    half = HEAD_DIM // 2
    frequency = 10000.0 ** (-jnp.arange(half, dtype=jnp.float32) / half)
    angle = position.astype(jnp.float32)[..., None] * frequency
    return (jnp.cos(angle), jnp.sin(angle))


def split_factors(factors):
    mix_width = HEADS * KV_RANK
    base_width = KV_RANK * HEAD_DIM
    count, rows = (factors.shape[0], factors.shape[1])
    key_mix = factors[..., :mix_width].reshape(count, rows, HEADS, KV_RANK)
    key_base = factors[..., mix_width : mix_width + base_width].reshape(
        count, rows, KV_RANK, HEAD_DIM
    )
    value_mix = factors[..., mix_width + base_width : 2 * mix_width + base_width].reshape(
        count, rows, HEADS, KV_RANK
    )
    value_base = factors[..., 2 * mix_width + base_width :].reshape(count, rows, KV_RANK, HEAD_DIM)
    return (key_mix, key_base, value_mix, value_base)


def pair_gradient(hidden_grad, gate, lifted):
    sigmoid = jax.nn.sigmoid(gate)
    gate_grad = hidden_grad * lifted * (sigmoid * (1.0 + gate * (1.0 - sigmoid)))
    lift_grad = hidden_grad * (gate * sigmoid)
    return jnp.concatenate([gate_grad, lift_grad], axis=-1).astype(jnp.bfloat16)


def body(
    tokens,
    lengths,
    cotangent,
    first_gain,
    query_heads,
    query_basis,
    key_heads,
    key_basis,
    value_heads,
    value_basis,
    output_weight,
    second_gain,
    gate_weight,
    up_weight,
    down_projection_weight,
):
    local, batch_rows, width = tokens.shape
    total = local * lax.axis_size("wide")
    offset = lax.axis_index("wide") * local
    places = jnp.arange(total, dtype=jnp.int32)
    segment, position, valid = jax.vmap(row_layout, in_axes=(0, None))(lengths, places)
    own_places = offset + jnp.arange(local, dtype=jnp.int32)
    own_segment = lax.dynamic_slice_in_dim(segment, offset, local, 1)
    own_position = lax.dynamic_slice_in_dim(position, offset, local, 1)
    own_valid = lax.dynamic_slice_in_dim(valid, offset, local, 1)
    cosine, sine = rope_tables(jnp.transpose(own_position))
    cosine = cosine[:, :, None, :]
    sine = sine[:, :, None, :]
    keep_rows = jnp.transpose(own_valid)[:, :, None]
    scale = HEAD_DIM ** (-0.5)
    block_rows = min(512, total)
    block_count = total // block_rows
    mix_width = HEADS * KV_RANK
    base_width = KV_RANK * HEAD_DIM
    flat_rows = local * batch_rows
    inputs = tokens.astype(jnp.float32)
    first_scale = rms_scale(inputs)
    normed = (inputs * first_scale * first_gain).astype(jnp.bfloat16)
    flat = normed.reshape(flat_rows, width)
    query_mix = jnp.dot(flat, query_heads, preferred_element_type=jnp.float32).reshape(
        local, batch_rows, HEADS, Q_RANK
    )
    query_raw = jnp.dot(flat, query_basis, preferred_element_type=jnp.float32).reshape(
        local, batch_rows, Q_RANK, HEAD_DIM
    )
    query_base = rotate(query_raw, cosine, sine)
    factor_weight = jnp.concatenate([key_heads, key_basis, value_heads, value_basis], axis=1)
    factor_raw = jnp.dot(flat, factor_weight, preferred_element_type=jnp.float32).reshape(
        local, batch_rows, -1
    )
    key_roped = rotate(
        factor_raw[..., mix_width : mix_width + base_width].reshape(
            local, batch_rows, KV_RANK, HEAD_DIM
        ),
        cosine,
        sine,
    ).reshape(local, batch_rows, base_width)
    factors = jnp.concatenate(
        [factor_raw[..., :mix_width], key_roped, factor_raw[..., mix_width + base_width :]], axis=-1
    ).astype(jnp.bfloat16)
    every = lax.all_gather(factors, "wide", axis=0, tiled=True)
    key_mix, key_base, value_mix, value_base = split_factors(every)
    keys = (
        jnp.einsum("trhk,trkd->trhd", key_mix, key_base, preferred_element_type=jnp.float32)
        / KV_RANK
    ).astype(jnp.bfloat16)
    values = (
        jnp.einsum("trhk,trkd->trhd", value_mix, value_base, preferred_element_type=jnp.float32)
        / KV_RANK
    ).astype(jnp.bfloat16)
    query = (
        jnp.einsum(
            "trhk,trkd->trhd",
            query_mix,
            query_base,
            precision=highest,
            preferred_element_type=jnp.float32,
        )
        / Q_RANK
    ).astype(jnp.bfloat16)

    def block_view(block):
        start = block * block_rows
        key_places = start + jnp.arange(block_rows, dtype=jnp.int32)
        key_segment = lax.dynamic_slice_in_dim(segment, start, block_rows, 1)
        key_valid = lax.dynamic_slice_in_dim(valid, start, block_rows, 1)
        causal = key_places[None, :] <= own_places[:, None]
        itself = key_places[None, :] == own_places[:, None]
        allowed = (
            causal[None]
            & (own_segment[:, :, None] == key_segment[:, None, :])
            & (key_valid[:, None, :] | itself[None])
        )
        key_block = lax.dynamic_slice_in_dim(keys, start, block_rows, 0)
        value_block = lax.dynamic_slice_in_dim(values, start, block_rows, 0)
        product = (
            jnp.einsum("qrhd,krhd->rhqk", query, key_block, preferred_element_type=jnp.float32)
            * scale
        )
        scores = jnp.where(allowed[:, None], product, masked_score)
        return (start, scores, key_block, value_block)

    def max_step(carry, block):
        top, mass = carry
        scores = block_view(block)[1]
        higher = jnp.maximum(top, jnp.max(scores, axis=-1))
        mass = mass * jnp.exp(top - higher) + jnp.sum(jnp.exp(scores - higher[..., None]), axis=-1)
        return ((higher, mass), None)

    start_top = jnp.full((batch_rows, HEADS, local), masked_score, jnp.float32)
    (top, mass), _ = lax.scan(
        max_step, (start_top, jnp.zeros_like(start_top)), jnp.arange(block_count)
    )
    log_total = top + jnp.log(mass)

    def out_step(carry, block):
        _, scores, _, value_block = block_view(block)
        chances = jnp.exp(scores - log_total[..., None]).astype(jnp.bfloat16)
        return (
            carry
            + jnp.einsum(
                "rhqk,krhd->qrhd", chances, value_block, preferred_element_type=jnp.float32
            ),
            None,
        )

    attended, _ = lax.scan(
        out_step,
        jnp.zeros((local, batch_rows, HEADS, HEAD_DIM), jnp.float32),
        jnp.arange(block_count),
    )
    mixed = attended.astype(jnp.bfloat16).reshape(flat_rows, HEADS * HEAD_DIM)
    hidden_state = inputs + jnp.dot(
        mixed, output_weight, preferred_element_type=jnp.float32
    ).reshape(local, batch_rows, width)
    second_scale = rms_scale(hidden_state)
    normed_second = (hidden_state * second_scale * second_gain).astype(jnp.bfloat16)
    normalized_token_rows = lax.all_gather(normed_second, "wide", axis=0, tiled=True)
    gate_lifted_hidden = jnp.concatenate([gate_weight, up_weight], axis=1)
    hidden_width = gate_weight.shape[1]
    projected_output = jnp.einsum(
        "zec,cx->zex", normalized_token_rows, gate_lifted_hidden, preferred_element_type=jnp.float32
    )
    gate = projected_output[..., :hidden_width]
    lifted = projected_output[..., hidden_width:]
    silu_hidden_output = (jax.nn.silu(gate) * lifted).astype(jnp.bfloat16)
    sequence_portion = silu_hidden_output
    branch = lax.psum_scatter(
        jnp.einsum(
            "zyu,uv->zyv",
            sequence_portion,
            down_projection_weight,
            preferred_element_type=jnp.float32,
        ).astype(jnp.bfloat16),
        "wide",
        scatter_dimension=0,
        tiled=True,
    ).astype(jnp.float32)
    output = jnp.where(keep_rows, hidden_state + branch, 0.0).astype(jnp.bfloat16)
    upstream = jnp.where(keep_rows, cotangent.astype(jnp.float32), 0.0)
    upstream_low = upstream.astype(jnp.bfloat16)
    upstream_token_gradient = lax.all_gather(upstream_low, "wide", axis=0, tiled=True)
    hidden_grad = jnp.einsum(
        "ajg,vg->ajv",
        upstream_token_gradient,
        down_projection_weight,
        preferred_element_type=jnp.float32,
    )
    pair_product_gradient = pair_gradient(hidden_grad, gate, lifted)
    down_gradient = jnp.einsum(
        "imj,ima->ja",
        silu_hidden_output,
        upstream_token_gradient,
        preferred_element_type=jnp.float32,
    )
    pair_weight_grad = jnp.einsum(
        "ipl,ipj->lj",
        normalized_token_rows,
        pair_product_gradient,
        preferred_element_type=jnp.float32,
    )
    sequence_portion = pair_product_gradient
    second_normed_grad = lax.psum_scatter(
        jnp.einsum(
            "ivu,bu->ivb", sequence_portion, gate_lifted_hidden, preferred_element_type=jnp.float32
        ),
        "wide",
        scatter_dimension=0,
        tiled=True,
    )
    second_gain_partial = jnp.sum(second_normed_grad * (hidden_state * second_scale), axis=(0, 1))
    residual_grad = upstream + norm_backward(
        hidden_state, second_gain, second_scale, second_normed_grad
    )
    residual_low = residual_grad.astype(jnp.bfloat16).reshape(flat_rows, width)
    output_weight_grad = jnp.einsum(
        "tk,td->kd", mixed, residual_low, preferred_element_type=jnp.float32
    )
    mixed_grad = (
        jnp.einsum("td,kd->tk", residual_low, output_weight, preferred_element_type=jnp.float32)
        .astype(jnp.bfloat16)
        .reshape(local, batch_rows, HEADS, HEAD_DIM)
    )

    def delta_step(carry, block):
        _, scores, _, value_block = block_view(block)
        chances = jnp.exp(scores - log_total[..., None])
        pressure = jnp.einsum(
            "qrhd,krhd->rhqk", mixed_grad, value_block, preferred_element_type=jnp.float32
        )
        return (carry + jnp.sum(chances * pressure, axis=-1), None)

    delta, _ = lax.scan(
        delta_step, jnp.zeros((batch_rows, HEADS, local), jnp.float32), jnp.arange(block_count)
    )

    def grad_step(carry, block):
        start, scores, key_block, value_block = block_view(block)
        chances = jnp.exp(scores - log_total[..., None])
        pressure = jnp.einsum(
            "qrhd,krhd->rhqk", mixed_grad, value_block, preferred_element_type=jnp.float32
        )
        score_grad = (chances * (pressure - delta[..., None])).astype(jnp.bfloat16)
        carry = (
            carry
            + jnp.einsum(
                "rhqk,krhd->qrhd", score_grad, key_block, preferred_element_type=jnp.float32
            )
            * scale
        )
        key_grad = (
            jnp.einsum("rhqk,qrhd->krhd", score_grad, query, preferred_element_type=jnp.float32)
            * scale
        )
        value_grad = jnp.einsum(
            "rhqk,qrhd->krhd",
            chances.astype(jnp.bfloat16),
            mixed_grad,
            preferred_element_type=jnp.float32,
        )
        block_mix, block_base, block_vmix, block_vbase = split_factors(
            lax.dynamic_slice_in_dim(every, start, block_rows, 0).astype(jnp.float32)
        )
        key_mix_grad = (
            jnp.einsum("krhd,krcd->krhc", key_grad, block_base, precision=highest) / KV_RANK
        )
        key_base_grad = (
            jnp.einsum("krhc,krhd->krcd", block_mix, key_grad, precision=highest) / KV_RANK
        )
        value_mix_grad = (
            jnp.einsum("krhd,krcd->krhc", value_grad, block_vbase, precision=highest) / KV_RANK
        )
        value_base_grad = (
            jnp.einsum("krhc,krhd->krcd", block_vmix, value_grad, precision=highest) / KV_RANK
        )
        block_grad = jnp.concatenate(
            [
                key_mix_grad.reshape(block_rows, batch_rows, mix_width),
                key_base_grad.reshape(block_rows, batch_rows, base_width),
                value_mix_grad.reshape(block_rows, batch_rows, mix_width),
                value_base_grad.reshape(block_rows, batch_rows, base_width),
            ],
            axis=-1,
        )
        return (carry, block_grad)

    query_grad, factor_blocks = lax.scan(
        grad_step,
        jnp.zeros((local, batch_rows, HEADS, HEAD_DIM), jnp.float32),
        jnp.arange(block_count),
    )
    factor_grads = factor_blocks.reshape(total, batch_rows, 2 * mix_width + 2 * base_width)
    own_factor_grads = lax.psum_scatter(
        factor_grads.astype(jnp.bfloat16), "wide", scatter_dimension=0, tiled=True
    ).astype(jnp.float32)
    key_base_back = rotate(
        own_factor_grads[..., mix_width : mix_width + base_width].reshape(
            local, batch_rows, KV_RANK, HEAD_DIM
        ),
        cosine,
        -sine,
    ).reshape(local, batch_rows, base_width)
    factor_low = (
        jnp.concatenate(
            [
                own_factor_grads[..., :mix_width],
                key_base_back,
                own_factor_grads[..., mix_width + base_width :],
            ],
            axis=-1,
        )
        .astype(jnp.bfloat16)
        .reshape(flat_rows, -1)
    )
    mix_grad = jnp.einsum("trhd,trcd->trhc", query_grad, query_base, precision=highest) / Q_RANK
    base_roped_grad = (
        jnp.einsum("trhc,trhd->trcd", query_mix, query_grad, precision=highest) / Q_RANK
    )
    base_grad = rotate(base_roped_grad, cosine, -sine)
    mix_low = mix_grad.astype(jnp.bfloat16).reshape(flat_rows, HEADS * Q_RANK)
    base_low = base_grad.astype(jnp.bfloat16).reshape(flat_rows, Q_RANK * HEAD_DIM)
    query_heads_grad = jnp.einsum("tk,tf->kf", flat, mix_low, preferred_element_type=jnp.float32)
    query_basis_grad = jnp.einsum("tk,tf->kf", flat, base_low, preferred_element_type=jnp.float32)
    factor_weight_grad = jnp.einsum(
        "tk,tf->kf", flat, factor_low, preferred_element_type=jnp.float32
    )
    first_normed_grad = (
        jnp.einsum("tf,kf->tk", mix_low, query_heads, preferred_element_type=jnp.float32)
        + jnp.einsum("tf,kf->tk", base_low, query_basis, preferred_element_type=jnp.float32)
        + jnp.einsum("tf,kf->tk", factor_low, factor_weight, preferred_element_type=jnp.float32)
    ).reshape(local, batch_rows, width)
    first_gain_partial = jnp.sum(first_normed_grad * (inputs * first_scale), axis=(0, 1))
    tokens_gradient = residual_grad + norm_backward(
        inputs, first_gain, first_scale, first_normed_grad
    )
    key_heads_grad = factor_weight_grad[:, :mix_width]
    key_basis_grad = factor_weight_grad[:, mix_width : mix_width + base_width]
    value_heads_grad = factor_weight_grad[:, mix_width + base_width : 2 * mix_width + base_width]
    value_basis_grad = factor_weight_grad[:, 2 * mix_width + base_width :]
    (
        first_share,
        qheads_share,
        qbasis_share,
        kheads_share,
        kbasis_share,
        vheads_share,
        vbasis_share,
        output_share,
        second_share,
    ) = (
        lax.psum_scatter(
            first_gain_partial.astype(jnp.bfloat16), "wide", scatter_dimension=0, tiled=True
        ).astype(jnp.float32),
        lax.psum_scatter(
            query_heads_grad.astype(jnp.bfloat16), "wide", scatter_dimension=0, tiled=True
        ).astype(jnp.float32),
        lax.psum_scatter(
            query_basis_grad.astype(jnp.bfloat16), "wide", scatter_dimension=0, tiled=True
        ).astype(jnp.float32),
        lax.psum_scatter(
            key_heads_grad.astype(jnp.bfloat16), "wide", scatter_dimension=0, tiled=True
        ).astype(jnp.float32),
        lax.psum_scatter(
            key_basis_grad.astype(jnp.bfloat16), "wide", scatter_dimension=0, tiled=True
        ).astype(jnp.float32),
        lax.psum_scatter(
            value_heads_grad.astype(jnp.bfloat16), "wide", scatter_dimension=0, tiled=True
        ).astype(jnp.float32),
        lax.psum_scatter(
            value_basis_grad.astype(jnp.bfloat16), "wide", scatter_dimension=0, tiled=True
        ).astype(jnp.float32),
        lax.psum_scatter(
            output_weight_grad.astype(jnp.bfloat16), "wide", scatter_dimension=0, tiled=True
        ).astype(jnp.float32),
        lax.psum_scatter(
            second_gain_partial.astype(jnp.bfloat16), "wide", scatter_dimension=0, tiled=True
        ).astype(jnp.float32),
    )
    gate_share = pair_weight_grad[:, :hidden_width]
    lift_share = pair_weight_grad[:, hidden_width:]
    totals = (
        lax.psum(first_share.astype(jnp.bfloat16), "batch").astype(jnp.float32),
        lax.psum(qheads_share.astype(jnp.bfloat16), "batch").astype(jnp.float32),
        lax.psum(qbasis_share.astype(jnp.bfloat16), "batch").astype(jnp.float32),
        lax.psum(kheads_share.astype(jnp.bfloat16), "batch").astype(jnp.float32),
        lax.psum(kbasis_share.astype(jnp.bfloat16), "batch").astype(jnp.float32),
        lax.psum(vheads_share.astype(jnp.bfloat16), "batch").astype(jnp.float32),
        lax.psum(vbasis_share.astype(jnp.bfloat16), "batch").astype(jnp.float32),
        lax.psum(output_share.astype(jnp.bfloat16), "batch").astype(jnp.float32),
        lax.psum(second_share.astype(jnp.bfloat16), "batch").astype(jnp.float32),
        lax.psum(gate_share.astype(jnp.bfloat16), "batch").astype(jnp.float32),
        lax.psum(lift_share.astype(jnp.bfloat16), "batch").astype(jnp.float32),
        lax.psum(down_gradient.astype(jnp.bfloat16), "batch").astype(jnp.float32),
    )
    return (
        output,
        tokens_gradient,
        totals[0],
        totals[1],
        totals[2],
        totals[3],
        totals[4],
        totals[5],
        totals[6],
        totals[7],
        totals[8],
        totals[9],
        totals[10],
        totals[11],
    )


def solution(mesh):
    return jax.shard_map(
        body,
        mesh=mesh,
        in_specs=(
            P("wide", "batch", None),
            P("batch", None),
            P("wide", "batch", None),
            P(),
            P(),
            P(),
            P(),
            P(),
            P(),
            P(),
            P(),
            P(),
            P(None, "wide"),
            P(None, "wide"),
            P("wide", None),
        ),
        out_specs=(
            P("wide", "batch", None),
            P("wide", "batch", None),
            P("wide"),
            P("wide", None),
            P("wide", None),
            P("wide", None),
            P("wide", None),
            P("wide", None),
            P("wide", None),
            P("wide", None),
            P("wide"),
            P(None, "wide"),
            P(None, "wide"),
            P("wide", None),
        ),
        check_vma=False,
    )
```

profile of v0, /device:TPU:8, one launch (start us, length us, event | category | flops | bytes accessed | tf_op | source)
XLA Modules:
  0.0 1633.9 jit_solution(7853648352892075791)
XLA Ops:
  97.0 18.3 %copy.329 = bf16[2048,2,16,64]{0,3,2,1:T(8,128)(2,1)} copy(bf16[2048,2,16,64]{3,2,1,0:T(8,128)(2,1)} %multiply_convert_fusion) | data formatting | bytes 16777216
  115.3 89.6 %while.48 = (s32[]{:T(128)}, f32[2,16,256]{2,1,0:T(8,128)S(1)}, f32[2,16,256]{2,1,0:T(8,128)S(1)}, s32[4]{0:T(128)S(1)}, s32[2,256]{1,0:T(2,128)S(1)}, /*index=5...) while((s32[]{:T(128)}, f32[2,16,256]{2,1,0:T(8,128)S(1)}, ...), condition=%wide.region_7.8_spmd.clone, body=%wide.region_4.7_spmd.clone.sunk | while | flops 567583488 | bytes 38460644 | solution.py:184
  215.8 18.3 %copy.328 = bf16[2048,2,16,64]{0,3,2,1:T(8,128)(2,1)} copy(bf16[2048,2,16,64]{3,2,1,0:T(8,128)(2,1)} %multiply_convert_fusion.1) | data formatting | bytes 16777216
  234.8 48.6 %while.49 = (s32[]{:T(128)}, f32[256,2,16,64]{0,3,2,1:T(8,128)}, s32[4]{0:T(128)S(1)}, bf16[2048,2,16,64]{0,3,2,1:T(8,128)(2,1)}, s32[2,256]{1,0:T(2,128)S(1)}, ...) while((s32[]{:T(128)}, f32[256,2,16,64]{0,3,2,1:T(8,128)}, ...), condition=%wide.region_9.10_spmd.clone, body=%wide.region_8.9_spmd.clone.sunk | while | flops 1092879104 | bytes 10543848 | solution.py:200
  291.9 51.9 %all-gather.6.cloned.1.call-done = bf16[2048,2,1024]{2,0,1:T(8,128)(2,1)} async-done(((bf16[256,2,1024]{2,0,1:T(8,128)(2,1)}), bf16[2048,2,1024]{2,0,1:T(8,128)(2,1)}) %all-gather.6.cloned.1.call-update) | async-done | bytes 8388624 | tf_op jit(solution)/shard_map/all_gather | solution.py:211
  343.9 11.8 fusion.91
  355.6 45.1 %all-gather.8.cloned.1.call-done = bf16[2048,2,1024]{2,0,1:T(8,128)(2,1)} async-done(((bf16[256,2,1024]{2,0,1:T(8,128)(2,1)}), bf16[2048,2,1024]{2,0,1:T(8,128)(2,1)}) %all-gather.8.cloned.1.call-update) | async-done | bytes 8388624 | tf_op jit(solution)/shard_map/all_gather | solution.py:235
  424.5 116.0 %reduce-scatter.23.cloned.1.call-done = f32[256,2,1024]{2,0,1:T(8,128)} async-done(((f32[2048,2,1024]{2,0,1:T(8,128)}), f32[256,2,1024]{2,0,1:T(8,128)}) %reduce-scatter.23.cloned.1.call-update) | async-done | bytes 2097168 | tf_op jit(solution)/shard_map/reduce_scatter | solution.py:256
  559.7 62.4 %while.50 = (s32[]{:T(128)}, f32[2,16,256]{2,1,0:T(8,128)}, s32[4]{0:T(128)S(1)}, s32[2,256]{1,0:T(2,128)S(1)}, s32[2,2048]{1,0:T(2,128)}, /*index=5*/pred[2,204...) while((s32[]{:T(128)}, f32[2,16,256]{2,1,0:T(8,128)}, ...), condition=%wide.region_16.17_spmd.clone, body=%wide.region_14.16_spmd.clone.sunk | while | flops 1096033024 | bytes 41082104 | solution.py:286
  622.1 464.1 %while.51 = (s32[]{:T(128)}, f32[256,2,16,64]{0,3,2,1:T(8,128)S(1)}, bf16[4,512,2,320]{1,3,2,0:T(8,128)(2,1)}, s32[4]{0:T(128)S(1)}, bf16[2048,2,16,64]{0,3,2,1:...) while((s32[]{:T(128)}, ...), condition=%wide.region_18.19_spmd.clone, body=%wide.region_17.18_spmd.clone.sunk | while | flops 2834170624 | bytes 175758848 | solution.py:340
  665.2 12.0 fusion.249
  703.7 11.0 convolution_multiply_fusion.11
  731.6 11.0 convolution_multiply_fusion.9
  773.9 12.0 fusion.249
  812.4 11.0 convolution_multiply_fusion.11
  840.3 11.0 convolution_multiply_fusion.9
  882.7 12.0 fusion.249
  921.2 11.0 convolution_multiply_fusion.11
  949.1 11.0 convolution_multiply_fusion.9
  991.5 12.0 fusion.249
  1030.0 11.0 convolution_multiply_fusion.11
  1057.9 11.0 convolution_multiply_fusion.9
  1118.7 14.9 reduce-scatter.25.cloned.1.call-done
  1211.9 12.7 all-reduce.2
  1227.2 16.5 %reduce-scatter.33.cloned.1.call-done = bf16[128,32]{1,0:T(8,128)(2,1)} async-done(((bf16[1024,32]{1,0:T(8,128)(2,1)}), bf16[128,32]{1,0:T(8,128)(2,1)}) %reduce-scatter.33.cloned.1.call-update) | async-done | bytes 8208
  1245.2 35.5 %reduce-scatter.39.cloned.1.call-done = bf16[128,128]{1,0:T(8,128)(2,1)} async-done(((bf16[1024,128]{1,0:T(8,128)(2,1)}), bf16[128,128]{1,0:T(8,128)(2,1)}) %reduce-scatter.39.cloned.1.call-update) | async-done | bytes 32784
  1282.2 35.1 %reduce-scatter.35.cloned.1.call-done = bf16[128,128]{1,0:T(8,128)(2,1)} async-done(((bf16[1024,128]{1,0:T(8,128)(2,1)}), bf16[128,128]{1,0:T(8,128)(2,1)}) %reduce-scatter.35.cloned.1.call-update) | async-done | bytes 32784
  1321.7 34.6 %reduce-scatter.27.cloned.1.call-done = bf16[128,384]{1,0:T(8,128)(2,1)} async-done(((bf16[1024,384]{1,0:T(8,128)(2,1)}), bf16[128,384]{1,0:T(8,128)(2,1)}) %reduce-scatter.27.cloned.1.call-update) | async-done | bytes 98320 | tf_op jit(solution)/shard_map/reduce_scatter | solution.py:410
  1356.3 44.8 %reduce-scatter.29.cloned.1.call-done = bf16[128,1024]{1,0:T(8,128)(2,1)} async-done(((bf16[1024,1024]{1,0:T(8,128)(2,1)}), bf16[128,1024]{1,0:T(8,128)(2,1)}) %reduce-scatter.29.cloned.1.call-update) | async-done | bytes 262160 | tf_op jit(solution)/shard_map/reduce_scatter | solution.py:425
  1401.1 74.7 %reduce-scatter.21.cloned.1.call-done = bf16[256,2,1024]{2,0,1:T(8,128)(2,1)} async-done(((bf16[2048,2,1024]{2,0,1:T(8,128)(2,1)}), bf16[256,2,1024]{2,0,1:T(8,128)(2,1)}) %reduce-scatter.21.cloned.1.call-update) | async-done | bytes 1048592 | tf_op jit(solution)/shard_map/reduce_scatter | solution.py:221
  1484.7 30.4 %all-reduce.8.cloned.1.call-done = (bf16[128,128]{0,1:T(8,128)(2,1)}, bf16[128,128]{0,1:T(8,128)(2,1)}, bf16[128]{0:T(256)(128)(2,1)}, bf16[128,96]{0,1:T(8,128)...) async-done(((bf16[128,128]{0,1:T(8,128)(2,1)}, bf16[128,128]{0,1:T(8,128)(2,1)}, bf16[128]{0:T(256)(128)(2,1)}, ...) | async-done | bytes 107024 | tf_op jit(solution)/shard_map/psum | solution.py:439
  1524.2 94.4 %all-reduce.10.cloned.1.call-done = (bf16[128,384]{1,0:T(8,128)(2,1)}, bf16[128,1024]{1,0:T(8,128)(2,1)}, bf16[1024,352]{0,1:T(8,128)(2,1)}, bf16[1024,352]{0,1:T(8,128)(2,1)}, bf16[352,1024]{1,0:T(8,128)(2,1)}) async-done(((bf16[128,384]{1,0:T(8,128)(2,1)}, bf16[128,1024]{1,0:T(8,128)(2,1)}, bf16[1024,352]{0,1:T(8,128)(2,1)}, bf16[1024,352]{0,1:T(8,128)(2,1)}, bf16[352,1024]{1,0:T(8,128)(2,1)}), ...) | async-done | bytes 2523152 | tf_op jit(solution)/shard_map/psum | solution.py:437
  (602 shorter events, 785.5 us)
Async XLA Ops:
  7.2 278.1 %copy-start = (bf16[1024,1024]{1,0:T(8,128)(2,1)S(1)}, bf16[1024,1024]{1,0:T(8,128)(2,1)}, u32[]{:S(2)}) copy-start(bf16[1024,1024]{1,0:T(8,128)(2,1)} %param.33) | copy-start | bytes 6291460
  7.2 49.8 %all-gather.4.cloned.1.call-start = ((), (), s32[]{:S(2)}) async-start(), calls=%async_computation.10 | async-start | bytes 2949120 | tf_op jit(solution)/shard_map/all_gather | solution.py:134
  25.2 318.7 %all-gather.6.cloned.1.call-start = ((), (), s32[]{:S(2)}) async-start(), calls=%async_computation.11 | async-start | bytes 9437184 | tf_op jit(solution)/shard_map/all_gather | solution.py:211
  286.8 257.3 %copy-start.53 = (f32[256,2]{0,1:T(2,128)}, f32[256,2]{0,1:T(2,128)S(1)}, u32[]{:S(2)}) copy-start(f32[256,2]{0,1:T(2,128)S(1)} %get-tuple-element.911) | copy-start | bytes 6148
  286.8 257.3 %copy-start.58 = (f32[256,2]{0,1:T(2,128)}, f32[256,2]{0,1:T(2,128)S(1)}, u32[]{:S(2)}) copy-start(f32[256,2]{0,1:T(2,128)S(1)} %get-tuple-element.910) | copy-start | bytes 6148
  289.3 111.5 %all-gather.8.cloned.1.call-start = ((), (), s32[]{:S(2)}) async-start(), calls=%async_computation.13 | async-start | bytes 9437184 | tf_op jit(solution)/shard_map/all_gather | solution.py:235
  289.4 254.7 %copy-start.62 = (pred[256,2]{0,1:T(4,128)(4,1)}, pred[256,2]{0,1:T(4,128)(4,1)S(1)}, u32[]{:S(2)}) copy-start(pred[256,2]{0,1:T(4,128)(4,1)S(1)} %dynamic-slice_bitcast_fusion) | copy-start | bytes 1540
  291.9 248.7 %reduce-scatter.23.cloned.1.call-start = ((), (), s32[]{:S(2)}) async-start(), calls=%async_computation.14 | async-start | bytes 18874368 | tf_op jit(solution)/shard_map/reduce_scatter | solution.py:256
  400.8 13.3 copy-start.67
  400.8 13.3 copy-start.68
  424.4 709.2 %reduce-scatter.25.cloned.1.call-start = ((), (), s32[]{:S(2)}) async-start(), calls=%async_computation.15 | async-start | bytes 2949120 | tf_op jit(solution)/shard_map/reduce_scatter | solution.py:346
  559.7 62.5 %copy-start.4 = (f32[256,2,16,64]{0,3,2,1:T(8,128)S(1)}, f32[256,2,16,64]{0,3,2,1:T(8,128)}, u32[]{:S(2)}) copy-start(f32[256,2,16,64]{0,3,2,1:T(8,128)} %custom-call.4) | copy-start | bytes 6291460
  1089.8 111.5 %reduce-scatter.31.cloned.1.call-start = ((), (), s32[]{:S(2)}) async-start(), calls=%async_computation.18 | async-start | bytes 294912
  1115.9 19.3 %copy-start.25 = (f32[256,2,32]{2,1,0:T(2,128)S(1)}, f32[256,2,32]{2,1,0:T(2,128)}, u32[]{:S(2)}) copy-start(f32[256,2,32]{2,1,0:T(2,128)} %copy-done.24) | copy-start | bytes 196612
  1116.0 19.3 %copy-start.34 = (f32[256,2,32]{2,1,0:T(2,128)S(1)}, f32[256,2,32]{2,1,0:T(2,128)}, u32[]{:S(2)}) copy-start(f32[256,2,32]{2,1,0:T(2,128)} %copy.354) | copy-start | bytes 196612
  1118.5 107.3 %reduce-scatter.37.cloned.1.call-start = ((), (), s32[]{:S(2)}) async-start(), calls=%async_computation.21 | async-start | bytes 294912
  1142.3 101.5 %reduce-scatter.33.cloned.1.call-start = ((), (), s32[]{:S(2)}) async-start(), calls=%async_computation.19 | async-start | bytes 294912
  1152.0 128.7 %reduce-scatter.39.cloned.1.call-start = ((), (), s32[]{:S(2)}) async-start(), calls=%async_computation.22 | async-start | bytes 294912
  1152.9 164.3 %reduce-scatter.35.cloned.1.call-start = ((), (), s32[]{:S(2)}) async-start(), calls=%async_computation.20 | async-start | bytes 294912
  1154.1 202.2 %reduce-scatter.27.cloned.1.call-start = ((), (), s32[]{:S(2)}) async-start(), calls=%async_computation.16 | async-start | bytes 884736 | tf_op jit(solution)/shard_map/reduce_scatter | solution.py:410
  1159.2 241.9 %reduce-scatter.29.cloned.1.call-start = ((), (), s32[]{:S(2)}) async-start(), calls=%async_computation.17 | async-start | bytes 2359296 | tf_op jit(solution)/shard_map/reduce_scatter | solution.py:425
  1168.9 306.9 %reduce-scatter.21.cloned.1.call-start = ((), (), s32[]{:S(2)}) async-start(), calls=%async_computation.12 | async-start | bytes 9437184 | tf_op jit(solution)/shard_map/reduce_scatter | solution.py:221
  1178.2 336.9 %all-reduce.8.cloned.1.call-start = ((), (), s32[]{:S(2)}) async-start(), calls=%async_computation.23 | async-start | bytes 215040 | tf_op jit(solution)/shard_map/psum | solution.py:439
  1210.7 108.0 %copy-start.15 = (f32[256,2,1024]{2,1,0:T(2,128)}, f32[256,2,1024]{2,1,0:T(2,128)S(1)}, u32[]{:S(2)}) copy-start(f32[256,2,1024]{2,1,0:T(2,128)S(1)} %reshape.450) | copy-start | bytes 6291460
  1318.7 157.1 %copy-start.9 = (f32[256,2,1024]{2,0,1:T(8,128)S(1)}, f32[256,2,1024]{2,0,1:T(8,128)}, u32[]{:S(2)}) copy-start(f32[256,2,1024]{2,0,1:T(8,128)} %copy-done.7) | copy-start | bytes 6291460
  1318.7 157.1 %copy-start.52 = (f32[1024]{0:T(1024)S(1)}, f32[1024]{0:T(1024)}, u32[]{:S(2)}) copy-start(f32[1024]{0:T(1024)} %param.34) | copy-start | bytes 12292
  1318.7 157.1 %copy-start.54 = (f32[256,2]{0,1:T(2,128)S(1)}, f32[256,2]{0,1:T(2,128)}, u32[]{:S(2)}) copy-start(f32[256,2]{0,1:T(2,128)} %copy-done.53) | copy-start | bytes 6148
  1318.8 157.1 %copy-start.59 = (f32[256,2]{0,1:T(2,128)S(1)}, f32[256,2]{0,1:T(2,128)}, u32[]{:S(2)}) copy-start(f32[256,2]{0,1:T(2,128)} %copy-done.58) | copy-start | bytes 6148
  1318.8 157.1 %copy-start.61 = (f32[256,2]{0,1:T(2,128)S(1)}, f32[256,2]{0,1:T(2,128)}, u32[]{:S(2)}) copy-start(f32[256,2]{0,1:T(2,128)} %copy-done.60) | copy-start | bytes 6148
  1318.8 157.1 %copy-start.63 = (pred[256,2]{0,1:T(4,128)(4,1)S(1)}, pred[256,2]{0,1:T(4,128)(4,1)}, u32[]{:S(2)}) copy-start(pred[256,2]{0,1:T(4,128)(4,1)} %copy-done.62) | copy-start | bytes 1540
  1318.8 157.1 %copy-start.64 = (f32[256,2]{0,1:T(2,128)S(1)}, f32[256,2]{0,1:T(2,128)}, u32[]{:S(2)}) copy-start(f32[256,2]{0,1:T(2,128)} %get-tuple-element.908) | copy-start | bytes 6148
  1318.8 299.9 %all-reduce.10.cloned.1.call-start = ((), (), s32[]{:S(2)}) async-start(), calls=%async_computation.24 | async-start | bytes 5046272 | tf_op jit(solution)/shard_map/psum | solution.py:437
  (73 other events, 413.4 us)
Sparse Core Ops, SparseCore 0:
  25.3 31.6 all-gather.3
  289.4 54.3 all-gather.5
  346.3 54.3 all-gather.7
  424.5 115.9 reduce-scatter.22
  1089.9 43.6 reduce-scatter.24
  1136.5 33.5 reduce-scatter.30
  1173.5 33.5 reduce-scatter.36
  1210.1 33.5 reduce-scatter.32
  1247.1 33.5 reduce-scatter.38
  1283.6 33.6 reduce-scatter.34
  1321.3 34.9 reduce-scatter.26
  1359.8 41.2 reduce-scatter.28
  1404.5 71.2 reduce-scatter.20
  1479.9 35.1 all-reduce.7
  1518.3 100.3 all-reduce.9
where the time goes:
time: 1650 us; the launch traced here: 1630 us
  waiting for transfers between devices  597 us (36%)
  matrix products  540 us (33%)
  local copies, waits for them, and re-layouts  319 us (19%)
  other arithmetic  107 us (6%)
  loops' own time  41.3 us (3%)
    reduce_scatter x1, waiting for transfers between devices, body(): lax.psum_scatter(jnp.einsum('ivu,bu->ivb', sequence_portion, gate_lifted_...  116 us
    dot_general x12, matrix products, block_view(): jnp.einsum('qrhd,krhd->rhqk', query, key_block, preferred_element_type=jn...  110 us
    psum x1, waiting for transfers between devices, body(): lax.psum(qbasis_share.astype(jnp.bfloat16), 'batch').astype(jnp.float32)  94.4 us
    unnamed x20, waiting for transfers between devices  87.3 us
    unnamed x168, local copies, waits for them, and re-layouts  78.1 us
    reduce_scatter x1, waiting for transfers between devices, body(): lax.psum_scatter(jnp.einsum('zyu,uv->zyv', sequence_portion, down_project...  74.7 us
    all_gather x1, waiting for transfers between devices, body(): lax.all_gather(normed_second, 'wide', axis=0, tiled=True)  51.9 us
    dot_general x4, matrix products, grad_step(): jnp.einsum('rhqk,qrhd->krhd', chances.astype(jnp.bfloat16), mixed_grad, p...  48.1 us
  transfers between devices with their start and end apart: 15, of which 13 were waited for; matrix products, arithmetic and copies ran while one was open for 10% of the time, Pallas kernels for 0%

commit v1 on v0

--- a/solution.py
+++ b/solution.py
@@ -1,12 +1,625 @@
+import functools
+
 import jax
 import jax.numpy as jnp
 from jax import lax
+from jax.experimental import pallas as pl
+from jax.experimental.pallas import tpu as pltpu
 from jax.sharding import PartitionSpec as P
 
 HEADS = 16
 HEAD_DIM = 64
 Q_RANK = 6
 KV_RANK = 2
+HALF = HEAD_DIM // 2
+MIX = HEADS * KV_RANK
+BASE = KV_RANK * HEAD_DIM
+FACTORS = 2 * MIX + 2 * BASE
+QMIX = HEADS * Q_RANK
+QBASE = Q_RANK * HEAD_DIM
+QUAD = 4
+QUADS = HEADS // QUAD
+QW = QUAD * HEAD_DIM
+TILE = 128
+F32 = jnp.float32
+BF16 = jnp.bfloat16
+NEG = -1e30
+MIB = 1 << 20
+
+
+def mm(a, b):
+    return jnp.dot(a, b, preferred_element_type=F32)
+
+
+def mm_nt(a, b):
+    return lax.dot_general(a, b, (((1,), (1,)), ((), ())), preferred_element_type=F32)
+
+
+def mm_tn(a, b):
+    return lax.dot_general(a, b, (((0,), (0,)), ((), ())), preferred_element_type=F32)
+
+
+def whole(count):
+    return [pl.BlockSpec(memory_space=pltpu.VMEM)] * count
+
+
+def streamed(shape):
+    return pl.BlockSpec(shape, lambda *_, rank=len(shape): (0,) * rank)
+
+
+def kernel_call(
+    kernel, name, outs, scratch, smem, limit, micros, *args, kept=(), far=(), aliases={}
+):
+    specs = [
+        pl.BlockSpec(memory_space=pltpu.SMEM)
+        if i < smem
+        else streamed(arg.shape)
+        if i in far
+        else pl.BlockSpec(memory_space=pltpu.VMEM)
+        for i, arg in enumerate(args)
+    ]
+    return pl.pallas_call(
+        kernel,
+        out_shape=tuple(
+            pltpu.HBM(s, t) if i in kept else jax.ShapeDtypeStruct(s, t)
+            for i, (s, t) in enumerate(outs)
+        ),
+        in_specs=specs,
+        out_specs=[
+            streamed(s) if i in kept else pl.BlockSpec(memory_space=pltpu.VMEM)
+            for i, (s, _) in enumerate(outs)
+        ],
+        scratch_shapes=scratch,
+        compiler_params=pltpu.CompilerParams(vmem_limit_bytes=limit * MIB),
+        cost_estimate=pl.CostEstimate(
+            flops=int(micros * 1e9), transcendentals=0, bytes_accessed=int(micros * 1e6)
+        ),
+        input_output_aliases=aliases,
+        name=name,
+    )(
+        *(
+            pltpu.with_memory_space_constraint(arg, pltpu.HBM) if i in far else arg
+            for i, arg in enumerate(args)
+        )
+    )
+
+
+def project_kernel(
+    x_ref, gain_ref, qh_ref, qb_ref, kh_ref, kb_ref, vh_ref, vb_ref, cos_ref, sin_ref,
+    fac_ref, qt_ref, qmix_ref, qbase_ref, normed_ref,
+):
+    x = x_ref[...].astype(F32)
+    scale = lax.rsqrt(jnp.mean(x * x, axis=-1, keepdims=True) + 1e-06)
+    normed = (x * scale * gain_ref[...]).astype(BF16)
+    normed_ref[...] = normed
+    cos = cos_ref[...]
+    sin = sin_ref[...]
+
+    def rope(v):
+        a, b = v[:HALF], v[HALF:]
+        return jnp.concatenate([a * cos - b * sin, a * sin + b * cos], axis=0)
+
+    kb = mm(normed, kb_ref[...]).T
+    fac_ref[0:MIX, :] = mm_nt(kh_ref[...], normed).astype(BF16)
+    for r in range(KV_RANK):
+        at = MIX + r * HEAD_DIM
+        fac_ref[at : at + HEAD_DIM, :] = rope(kb[r * HEAD_DIM : (r + 1) * HEAD_DIM]).astype(BF16)
+    fac_ref[MIX + BASE : 2 * MIX + BASE, :] = mm_nt(vh_ref[...], normed).astype(BF16)
+    fac_ref[2 * MIX + BASE :, :] = mm(normed, vb_ref[...]).T.astype(BF16)
+    qmix = mm_nt(qh_ref[...], normed)
+    qmix_ref[...] = qmix
+    raw = mm(normed, qb_ref[...]).T
+    base = [rope(raw[r * HEAD_DIM : (r + 1) * HEAD_DIM]) for r in range(Q_RANK)]
+    for r in range(Q_RANK):
+        qbase_ref[r * HEAD_DIM : (r + 1) * HEAD_DIM, :] = base[r]
+    for h in range(HEADS):
+        out = None
+        for r in range(Q_RANK):
+            part = qmix[h * Q_RANK + r : h * Q_RANK + r + 1, :] * base[r]
+            out = part if out is None else out + part
+        qt_ref[h * HEAD_DIM : (h + 1) * HEAD_DIM, :] = (
+            (out * (1.0 / Q_RANK)).astype(BF16) * (HEAD_DIM ** -0.5)
+        ).astype(BF16)
+
+
+def project(x, gain, weights, cos, sin):
+    local, d = x.shape
+    width = HEADS * HEAD_DIM
+    return kernel_call(
+        project_kernel,
+        "project",
+        (
+            ((FACTORS, local), BF16),
+            ((width, local), BF16),
+            ((QMIX, local), F32),
+            ((QBASE, local), F32),
+            ((local, d), BF16),
+        ),
+        [],
+        0,
+        16,
+        2,
+        x, gain, *weights, cos, sin,
+        kept=(1, 2, 3, 4),
+    )
+
+
+def materialize(fac, offset, head):
+    base = offset + MIX
+    out = None
+    for r in range(KV_RANK):
+        row = offset + head * KV_RANK + r
+        part = fac[row : row + 1, :] * fac[base + r * HEAD_DIM : base + (r + 1) * HEAD_DIM, :]
+        out = part if out is None else out + part
+    return (out * (1.0 / KV_RANK)).astype(BF16)
+
+
+def materialize_quad(fac, offset, quad):
+    return jnp.concatenate(
+        [materialize(fac, offset, quad * QUAD + i) for i in range(QUAD)], axis=0
+    )
+
+
+def each_block(me, lo, hi, slots, do):
+    for slot in range(slots):
+        kb = jnp.bitwise_xor(me, slot)
+        pl.when((kb >= lo) & (kb < hi))(functools.partial(do, slot, kb))
+
+
+def block_factors(slot, near, far):
+    return (far if slot & 1 else near)[slot >> 1].astype(F32)
+
+
+def forward_kernel(
+    span, qt_ref, near_ref, far_ref, info_ref, x_ref, wo_ref, gain_ref,
+    mixed_ref, out_t_ref, lse_ref, hidden_ref, n2_ref,
+    k_s, vt_s, qbd_s, acc_s, m_s, l_s, bias_s,
+):
+    slots, kb_size, _ = k_s.shape
+    count = qt_ref.shape[1]
+    lo, hi, me = span[0], span[1], span[2]
+
+    def prepare(slot, kb):
+        fac = block_factors(slot, near_ref, far_ref)
+        for quad in range(QUADS):
+            rows = slice(quad * QW, (quad + 1) * QW)
+            k_s[kb, :, rows] = materialize_quad(fac, 0, quad).T
+            vt_s[kb, rows, :] = materialize_quad(fac, MIX + BASE, quad)
+
+    each_block(me, lo, hi, slots, prepare)
+    qbd_s[...] = jnp.zeros_like(qbd_s)
+    for h in range(HEADS):
+        quad, i = h // QUAD, h % QUAD
+        qbd_s[quad, i * HEAD_DIM : (i + 1) * HEAD_DIM, i * count : (i + 1) * count] = qt_ref[
+            h * HEAD_DIM : (h + 1) * HEAD_DIM, :
+        ]
+    m_s[...] = jnp.full_like(m_s, NEG)
+    l_s[...] = jnp.zeros_like(l_s)
+    acc_s[...] = jnp.zeros_like(acc_s)
+    first = info_ref[0:1, :]
+    last = info_ref[1:2, :]
+
+    def step(kb, _):
+        places = kb * kb_size + lax.broadcasted_iota(jnp.int32, (kb_size, count), 0)
+        bias_s[...] = jnp.where((places >= first) & (places <= last), 0.0, NEG)
+        for quad in range(QUADS):
+            s = mm(k_s[kb, :, quad * QW : (quad + 1) * QW], qbd_s[quad])
+            ps = []
+            alphas = []
+            for i in range(QUAD):
+                h = quad * QUAD + i
+                sh = s[:, i * count : (i + 1) * count] + bias_s[...]
+                old = m_s[h : h + 1, :]
+                new = jnp.maximum(old, jnp.max(sh, axis=0, keepdims=True))
+                alpha = jnp.exp(old - new)
+                p = jnp.exp(sh - new)
+                m_s[h : h + 1, :] = new
+                l_s[h : h + 1, :] = l_s[h : h + 1, :] * alpha + jnp.sum(p, axis=0, keepdims=True)
+                ps.append(p.astype(BF16))
+                alphas.append(alpha)
+            for j in range(QUAD // 2):
+                both = jnp.concatenate(ps[2 * j : 2 * j + 2], axis=1)
+                at = quad * QW + j * 2 * HEAD_DIM
+                o = mm(vt_s[kb, at : at + 2 * HEAD_DIM, :], both)
+                for i in range(2):
+                    r = slice(at + i * HEAD_DIM, at + (i + 1) * HEAD_DIM)
+                    acc_s[r, :] = (
+                        acc_s[r, :] * alphas[2 * j + i]
+                        + o[i * HEAD_DIM : (i + 1) * HEAD_DIM, i * count : (i + 1) * count]
+                    )
+        return 0
+
+    lax.fori_loop(lo, hi, step, 0)
+    lse_ref[...] = m_s[...] + jnp.log(l_s[...])
+    for h in range(HEADS):
+        rows = slice(h * HEAD_DIM, (h + 1) * HEAD_DIM)
+        out_t_ref[rows, :] = acc_s[rows, :] * (1.0 / l_s[h : h + 1, :])
+
+    mixed = out_t_ref[...].astype(BF16).T
+    mixed_ref[...] = mixed
+    hidden = x_ref[...].astype(F32) + mm(mixed, wo_ref[...])
+    hidden_ref[...] = hidden
+    scale = lax.rsqrt(jnp.mean(hidden * hidden, axis=-1, keepdims=True) + 1e-06)
+    n2_ref[...] = (hidden * scale * gain_ref[...]).astype(BF16)
+
+
+def attend_forward(span, qt, near, far, info, x, wo, gain):
+    width, local = qt.shape
+    kb = local
+    blocks = 2 * near.shape[0]
+    d = x.shape[1]
+    return kernel_call(
+        forward_kernel,
+        "attend_forward",
+        (
+            ((local, width), BF16),
+            ((width, local), F32),
+            ((HEADS, local), F32),
+            ((local, d), F32),
+            ((local, d), BF16),
+        ),
+        [
+            pltpu.VMEM((blocks, kb, width), BF16),
+            pltpu.VMEM((blocks, width, kb), BF16),
+            pltpu.VMEM((QUADS, QW, QUAD * local), BF16),
+            pltpu.VMEM((width, local), F32),
+            pltpu.VMEM((HEADS, local), F32),
+            pltpu.VMEM((HEADS, local), F32),
+            pltpu.VMEM((kb, local), F32),
+        ],
+        1,
+        32,
+        10,
+        span, qt, near, far, info, x, wo, gain,
+        kept=(0, 1, 2, 3),
+    )
+
+
+def ffn_kernel(first, final, *refs):
+    at_y, n2_ref, up_ref, w_ref = refs[:4]
+    prev = None if first else refs[4]
+    sng_ref, branch_ref, sums = refs[-3:]
+    n2 = n2_ref[...]
+    up = up_ref[...]
+    hid = w_ref.shape[1]
+    gate = mm_nt(n2, w_ref[0])
+    lifted = mm_nt(n2, w_ref[1])
+    hidden_grad = mm_nt(up, w_ref[2])
+    sigmoid = jax.nn.sigmoid(gate)
+    silu = gate * sigmoid
+    act = (silu * lifted).astype(BF16)
+    gate_grad = (hidden_grad * lifted * (sigmoid * (1.0 + gate * (1.0 - sigmoid)))).astype(BF16)
+    lift_grad = (hidden_grad * silu).astype(BF16)
+    sng_ref[...] = (mm(gate_grad, w_ref[0]) + mm(lift_grad, w_ref[1])).astype(BF16)
+    branch_ref[...] = mm(act, w_ref[2]).astype(BF16)
+    for at, (left, right) in enumerate(((act, up), (gate_grad, n2), (lift_grad, n2))):
+        grad = mm_tn(left, right)
+        if not first:
+            grad = grad + prev[at]
+        if not final:
+            sums[at] = grad
+        else:
+            half = hid // 2
+            low = grad.astype(BF16)
+            sums[at_y[0], at] = low[:half]
+            sums[1 - at_y[0], at] = low[half:]
+
+
+def feed_forward(at_y, n2, up, weights, prev=None, final=False):
+    count, d = n2.shape
+    hid = weights.shape[1]
+    if final:
+        grads = (((2, 3, hid // 2, d), BF16),)
+    else:
+        grads = ((weights.shape, F32),)
+    args = (at_y, n2, up, weights) if prev is None else (at_y, n2, up, weights, prev)
+    return kernel_call(
+        functools.partial(ffn_kernel, prev is None, final),
+        "feed_forward",
+        (((count, d), BF16),) * 2 + grads,
+        [],
+        1,
+        19,
+        9,
+        *args,
+        kept=(1, 2) if final else (1,),
+        aliases={} if prev is None or final else {4: 2},
+    )
+
+
+def residual_kernel(
+    sa, sb, up_ref, hidden_ref, gain_ref, wo_ref, out_t_ref,
+    res_ref, low_ref, dot_ref, delta_ref, gain_out,
+):
+    sng = sa[...].astype(F32) + sb[...].astype(F32)
+    hidden = hidden_ref[...]
+    scale = lax.rsqrt(jnp.mean(hidden * hidden, axis=-1, keepdims=True) + 1e-06)
+    gain_out[...] = jnp.sum(sng * (hidden * scale), axis=0, keepdims=True)
+    weighted = sng * gain_ref[...]
+    inner = jnp.mean(hidden * weighted, axis=-1, keepdims=True)
+    res = up_ref[...].astype(F32) + scale * weighted - hidden * (scale * scale * scale) * inner
+    res_ref[...] = res
+    low = res.astype(BF16)
+    low_ref[...] = low
+    dot = mm_nt(wo_ref[...], low).astype(BF16)
+    dot_ref[...] = dot
+    for h in range(HEADS):
+        rows = slice(h * HEAD_DIM, (h + 1) * HEAD_DIM)
+        delta_ref[h : h + 1, :] = jnp.sum(
+            dot[rows].astype(F32) * out_t_ref[rows, :], axis=0, keepdims=True
+        )
+
+
+def residual(sa, sb, up, hidden, gain, wo, out_t, far=()):
+    local, d = hidden.shape
+    width = out_t.shape[0]
+    return kernel_call(
+        residual_kernel,
+        "residual",
+        (
+            ((local, d), F32),
+            ((local, d), BF16),
+            ((width, local), BF16),
+            ((HEADS, local), F32),
+            ((1, d), F32),
+        ),
+        [],
+        0,
+        16,
+        3,
+        sa, sb, up, hidden, gain, wo, out_t,
+        kept=(0,),
+        far=far,
+    )
+
+
+def backward_kernel(
+    span, qt_ref, near_ref, far_ref, info_ref, dot_ref, lse_ref, delta_ref,
+    qmix_ref, qbase_ref, cos_ref, sin_ref,
+    dnear_ref, dfar_ref, dq_ref,
+    k_s, kt_s, vt_s, dkt_s, dvt_s, qbd_s, qbdt_s, obd_s, obdt_s, dq_s, bias_s, lse_s, delta_s,
+):
+    slots, kb_size, _ = k_s.shape
+    count = qt_ref.shape[1]
+    lo, hi, me = span[0], span[1], span[2]
+    dnear_ref[...] = jnp.zeros_like(dnear_ref)
+    dfar_ref[...] = jnp.zeros_like(dfar_ref)
+
+    def prepare(slot, kb):
+        fac = block_factors(slot, near_ref, far_ref)
+        for quad in range(QUADS):
+            rows = slice(quad * QW, (quad + 1) * QW)
+            kt = materialize_quad(fac, 0, quad)
+            kt_s[kb, rows, :] = kt
+            k_s[kb, :, rows] = kt.T
+            vt_s[kb, rows, :] = materialize_quad(fac, MIX + BASE, quad)
+            dkt_s[kb, rows, :] = jnp.zeros((QW, kb_size), F32)
+            dvt_s[kb, rows, :] = jnp.zeros((QW, kb_size), F32)
+
+    each_block(me, lo, hi, slots, prepare)
+    qbdt_s[...] = jnp.zeros_like(qbdt_s)
+    obdt_s[...] = jnp.zeros_like(obdt_s)
+
+    for h in range(HEADS):
+        quad, i = h // QUAD, h % QUAD
+        to = slice(i * HEAD_DIM, (i + 1) * HEAD_DIM)
+        at = slice(i * count, (i + 1) * count)
+        rows = slice(h * HEAD_DIM, (h + 1) * HEAD_DIM)
+        qbdt_s[quad, to, at] = qt_ref[rows, :]
+        obdt_s[quad, to, at] = dot_ref[rows, :]
+    for quad in range(QUADS):
+        qbd_s[quad] = qbdt_s[quad].T
+        obd_s[quad] = obdt_s[quad].T
+    lse_t = lse_ref[:, :].T
+    delta_t = delta_ref[:, :].T
+    for h in range(HEADS):
+        lse_s[h] = jnp.broadcast_to(lse_t[:, h : h + 1], (count, TILE))
+        delta_s[h] = jnp.broadcast_to(delta_t[:, h : h + 1], (count, TILE))
+    dq_s[...] = jnp.zeros_like(dq_s)
+    info_t = info_ref[:, :].T
+    first = info_t[:, 0:1]
+    last = info_t[:, 1:2]
+
+    def step(kb, _):
+        places = kb * kb_size + lax.broadcasted_iota(jnp.int32, (count, kb_size), 1)
+        bias_s[...] = jnp.where((places >= first) & (places <= last), 0.0, NEG)
+        lane = lax.broadcasted_iota(jnp.int32, (count, QW), 1) // HEAD_DIM
+        for quad in range(QUADS):
+            rows = slice(quad * QW, (quad + 1) * QW)
+            s = mm(qbd_s[quad], kt_s[kb, rows, :])
+            dp = mm(obd_s[quad], vt_s[kb, rows, :])
+            ps = []
+            dss = []
+            for i in range(QUAD):
+                h = quad * QUAD + i
+                at = slice(i * count, (i + 1) * count)
+                lse = jnp.concatenate([lse_s[h]] * (kb_size // TILE), axis=1)
+                delta = jnp.concatenate([delta_s[h]] * (kb_size // TILE), axis=1)
+                p = jnp.exp((s[at] + bias_s[...]) - lse)
+                ps.append(p.astype(BF16))
+                dss.append((p * (dp[at] - delta)).astype(BF16))
+            p4 = jnp.concatenate(ps, axis=0)
+            ds4 = jnp.concatenate(dss, axis=0)
+            dkt_s[kb, rows, :] += mm(qbdt_s[quad], ds4)
+            dvt_s[kb, rows, :] += mm(obdt_s[quad], p4)
+            dq = mm(ds4, k_s[kb, :, rows])
+            out = dq[0:count]
+            for i in range(1, QUAD):
+                out = jnp.where(lane == i, dq[i * count : (i + 1) * count], out)
+            dq_s[:, rows] += out
+        return 0
+
+    lax.fori_loop(lo, hi, step, 0)
+    dqt = dq_s[...].T * (HEAD_DIM ** -0.5 / Q_RANK)
+    qmix = qmix_ref[:, :]
+    for h in range(HEADS):
+        part = dqt[h * HEAD_DIM : (h + 1) * HEAD_DIM, :]
+        dq_ref[h * Q_RANK : (h + 1) * Q_RANK, :] = jnp.concatenate(
+            [
+                jnp.sum(
+                    part * qbase_ref[r * HEAD_DIM : (r + 1) * HEAD_DIM, :],
+                    axis=0,
+                    keepdims=True,
+                )
+                for r in range(Q_RANK)
+            ],
+            axis=0,
+        )
+    cos = cos_ref[:, :]
+    sin = sin_ref[:, :]
+    for r in range(Q_RANK):
+        out = None
+        for h in range(HEADS):
+            row = h * Q_RANK + r
+            part = qmix[row : row + 1, :] * dqt[h * HEAD_DIM : (h + 1) * HEAD_DIM, :]
+            out = part if out is None else out + part
+        upper, lower = out[:HALF], out[HALF:]
+        at = QMIX + r * HEAD_DIM
+        dq_ref[at : at + HALF, :] = upper * cos + lower * sin
+        dq_ref[at + HALF : at + HEAD_DIM, :] = lower * cos - upper * sin
+
+    def fold(slot, kb):
+        fac = block_factors(slot, near_ref, far_ref)
+        to = dfar_ref if slot & 1 else dnear_ref
+        for offset, grad in ((0, dkt_s), (MIX + BASE, dvt_s)):
+            outs = [None] * KV_RANK
+            mixes = []
+            for h in range(HEADS):
+                g = grad[kb, h * HEAD_DIM : (h + 1) * HEAD_DIM, :] * (1.0 / KV_RANK)
+                for r in range(KV_RANK):
+                    at = offset + MIX + r * HEAD_DIM
+                    mixes.append(jnp.sum(g * fac[at : at + HEAD_DIM, :], axis=0, keepdims=True))
+                    row = offset + h * KV_RANK + r
+                    part = fac[row : row + 1, :] * g
+                    outs[r] = part if outs[r] is None else outs[r] + part
+            to[slot >> 1, offset : offset + MIX, :] = jnp.concatenate(mixes, axis=0).astype(BF16)
+            for r in range(KV_RANK):
+                at = offset + MIX + r * HEAD_DIM
+                to[slot >> 1, at : at + HEAD_DIM, :] = outs[r].astype(BF16)
+
+    each_block(me, lo, hi, slots, fold)
+
+
+def attend_backward(micros, span, qt, near, far, info, dot, lse, delta, qmix, qbase, cos, sin):
+    width, local = qt.shape
+    kb = local
+    blocks = 2 * near.shape[0]
+    return kernel_call(
+        backward_kernel,
+        "attend_backward",
+        (
+            (near.shape, BF16),
+            (near.shape, BF16),
+            ((QMIX + QBASE, local), F32),
+        ),
+        [
+            pltpu.VMEM((blocks, kb, width), BF16),
+            pltpu.VMEM((blocks, width, kb), BF16),
+            pltpu.VMEM((blocks, width, kb), BF16),
+            pltpu.VMEM((blocks, width, kb), F32),
+            pltpu.VMEM((blocks, width, kb), F32),
+            pltpu.VMEM((QUADS, QUAD * local, QW), BF16),
+            pltpu.VMEM((QUADS, QW, QUAD * local), BF16),
+            pltpu.VMEM((QUADS, QUAD * local, QW), BF16),
+            pltpu.VMEM((QUADS, QW, QUAD * local), BF16),
+            pltpu.VMEM((local, width), F32),
+            pltpu.VMEM((local, kb), F32),
+            pltpu.VMEM((HEADS, local, TILE), F32),
+            pltpu.VMEM((HEADS, local, TILE), F32),
+        ],
+        1,
+        56,
+        micros,
+        span, qt, near, far, info, dot, lse, delta, qmix, qbase, cos, sin,
+        far=(1, 6, 8, 9),
+    )
+
+
+def finish_kernel(*refs):
+    fa, f1, f2, f3, dq_ref, cos_ref, sin_ref, x_ref, gain_ref, res_ref = refs[:10]
+    weights = refs[10:16]
+    low_ref, grad_ref, gain_out = refs[16:]
+    total = (fa[...].astype(F32) + f1[...].astype(F32)) + (
+        f2[...].astype(F32) + f3[...].astype(F32)
+    )
+    cos = cos_ref[...]
+    sin = sin_ref[...]
+    query = QMIX + QBASE
+    low_ref[:query, :] = dq_ref[...].astype(BF16)
+    low_ref[query:, :] = total.astype(BF16)
+    for r in range(KV_RANK):
+        at = MIX + r * HEAD_DIM
+        a, b = total[at : at + HALF], total[at + HALF : at + HEAD_DIM]
+        to = query + at
+        low_ref[to : to + HALF, :] = (a * cos + b * sin).astype(BF16)
+        low_ref[to + HALF : to + HEAD_DIM, :] = (b * cos - a * sin).astype(BF16)
+    low = low_ref[...].T
+    grad = None
+    at = 0
+    for ref in weights:
+        if ref.shape[0] == x_ref.shape[1]:
+            count = ref.shape[1]
+            part = mm_nt(low[:, at : at + count], ref[...])
+        else:
+            count = ref.shape[0]
+            part = mm(low[:, at : at + count], ref[...])
+        grad = part if grad is None else grad + part
+        at += count
+    x = x_ref[...].astype(F32)
+    scale = lax.rsqrt(jnp.mean(x * x, axis=-1, keepdims=True) + 1e-06)
+    gain_out[...] = jnp.sum(grad * (x * scale), axis=0, keepdims=True)
+    weighted = grad * gain_ref[...]
+    inner = jnp.mean(x * weighted, axis=-1, keepdims=True)
+    grad_ref[...] = res_ref[...] + (scale * weighted - x * (scale * scale * scale) * inner)
+
+
+def finish(pieces, dq, cos, sin, x, gain, res, weights):
+    local, d = x.shape
+    return kernel_call(
+        finish_kernel,
+        "finish",
+        (
+            ((QMIX + QBASE + FACTORS, local), BF16),
+            ((local, d), F32),
+            ((1, d), F32),
+        ),
+        [],
+        0,
+        16,
+        2,
+        *pieces, dq, cos, sin, x, gain, res, *weights,
+    )
+
+
+def share_kernel(me, low0, low1, n0, n1, g0, g1, h0, h1, near_ref, far_ref, all_s):
+    rows = low0.shape[0]
+    all_s[:rows, :] = mm(
+        jnp.concatenate([low0[...], low1[...]], axis=1),
+        jnp.concatenate([n0[...], n1[...]], axis=0),
+    )
+    all_s[rows:, :] = jnp.concatenate(
+        [g0[...] + g1[...], h0[...] + h1[...], jnp.zeros((14, g0.shape[1]), F32)], axis=0
+    )
+    width = near_ref.shape[2]
+    for is_far, ref in ((0, near_ref), (1, far_ref)):
+        for slot in range(ref.shape[0]):
+            at = pl.multiple_of(jnp.bitwise_xor(me[0], 2 * slot + is_far) * width, width)
+            ref[slot] = all_s[:, pl.ds(at, width)].astype(BF16)
+
+
+def share(me, lows, normeds, first_gains, second_gains, slots):
+    rows = lows[0].shape[0] + 16
+    d = normeds[0].shape[1]
+    return kernel_call(
+        share_kernel,
+        "share",
+        (((slots // 2, rows, d // slots), BF16),) * 2,
+        [pltpu.VMEM((rows, d), F32)],
+        1,
+        16,
+        2,
+        me, *lows, *normeds, *first_gains, *second_gains,
+    )
 
 
 highest = lax.Precision.HIGHEST
@@ -70,7 +683,7 @@
     return jnp.concatenate([gate_grad, lift_grad], axis=-1).astype(jnp.bfloat16)
 
 
-def body(
+def general_body(
     tokens,
     lengths,
     cotangent,
@@ -463,42 +1076,307 @@
     )
 
 
+def partners(distance, count):
+    return [(i, i ^ distance) for i in range(count)]
+
+
+def fence(*values):
+    return lax.optimization_barrier(values)
+
+
+def after(value, *others):
+    return lax.optimization_barrier((value,) + others)[0]
+
+
+def body(
+    tokens,
+    lengths,
+    cotangent,
+    first_gain,
+    query_heads,
+    query_basis,
+    key_heads,
+    key_basis,
+    value_heads,
+    value_basis,
+    output_weight,
+    second_gain,
+    gate_weight,
+    up_weight,
+    down_projection_weight,
+):
+    local, rows, width = tokens.shape
+    wide = ("y", "x", "core")
+    n = lax.axis_size(wide)
+    depth = lax.axis_size("batch")
+    me = lax.axis_index(wide).astype(jnp.int32)
+    at_y = lax.axis_index("y").astype(jnp.int32).reshape(1)
+
+    def swap(value, distance):
+        return lax.ppermute(value, wide, partners(distance, n))
+
+    def swap_batch(value, distance):
+        return lax.ppermute(value, "batch", partners(distance, depth))
+
+    core, across, along, diagonal = 1, 2, 4, 6
+    chips = (across, along, diagonal)
+
+    def send_chips(value):
+        return [swap(value, distance) for distance in chips]
+
+    def send_slots(sums):
+        return [swap(sums[i + 1], chips[i]) for i in range(len(chips))]
+
+    def add(*values):
+        return sum(value.astype(F32) for value in values).astype(BF16)
+
+    places = me * local + jnp.arange(local, dtype=jnp.int32)
+    slots = lengths.shape[1]
+    upto = jnp.arange(slots)[:, None] >= jnp.arange(slots)[None, :]
+    ends = jnp.sum(jnp.where(upto[None], lengths[:, None, :], 0), axis=2)
+    passed = ends[:, None, :] <= places[None, :, None]
+    start = jnp.max(jnp.where(passed, ends[:, None, :], 0), axis=2)
+    valid = places[None, :] < ends[:, -1:]
+    position = places[None, :] - start
+    first_seen = jnp.where(valid, start, places[None, :])
+    frequency = 10000.0 ** (-jnp.arange(HALF, dtype=F32) / HALF)
+    angle = position.astype(F32)[:, None, :] * frequency[None, :, None]
+    cosine, sine = jnp.cos(angle), jnp.sin(angle)
+    info = jnp.stack([first_seen, jnp.broadcast_to(places, (rows, local))], axis=1)
+    info = jnp.concatenate([info, jnp.zeros((rows, 6, local), jnp.int32)], axis=1)
+    spans = jnp.stack(
+        [
+            jnp.min(first_seen, axis=1) // local,
+            jnp.broadcast_to(me + 1, (rows,)),
+            jnp.broadcast_to(me, (rows,)),
+        ],
+        axis=1,
+    ).astype(jnp.int32)
+
+    gain1 = first_gain.reshape(1, width)
+    gain2 = second_gain.reshape(1, width)
+    projections = (query_heads, query_basis, key_heads, key_basis, value_heads, value_basis)
+    narrow = tuple(w.T if w.shape[1] < TILE else w for w in projections)
+
+    xs = [tokens[:, b, :] for b in range(rows)]
+    projected = [project(xs[0], gain1, narrow, cosine[0], sine[0])]
+    sent0 = send_chips(projected[0][0])
+    x1 = after(xs[1], projected[0][0])
+    projected.append(project(x1, gain1, narrow, cosine[1], sine[1]))
+    sent1 = send_chips(projected[1][0])
+    own_weights = jnp.stack(
+        [after(gate_weight.T, projected[1][0]), up_weight.T, down_projection_weight]
+    )
+    other_weights = swap(own_weights, along)
+    near = jnp.stack([projected[0][0]] + [after(got, own_weights) for got in sent0])
+    far = swap(near, core)
+    gathered = [(near, far)]
+    seen = after(valid, near)
+    ups = [jnp.where(seen[b][:, None], cotangent[:, b, :], 0) for b in range(rows)]
+    up_pair = jnp.concatenate(ups, axis=0)
+    up_got = swap(up_pair, across)
+
+    def forward(b):
+        outs = attend_forward(
+            spans[b], projected[b][1], *gathered[b], info[b], xs[b], output_weight, gain2
+        )
+        return outs[:4], outs[4]
+
+    gathered[0] = (near, after(far, up_pair))
+    kept0, n20 = forward(0)
+    n20, up_got, *sent1 = fence(n20, up_got, *sent1)
+    n2_sent0 = swap(n20, across)
+    near = jnp.stack([projected[1][0]] + list(sent1))
+    far = swap(near, core)
+    up_near = [
+        jnp.concatenate([ups[b], up_got[b * local : (b + 1) * local]], axis=0)
+        for b in range(rows)
+    ]
+    near, far, *up_near = fence(near, far, *up_near)
+    gathered.append((near, far))
+    up_far = [swap(up_near[b], core) for b in range(rows)]
+    kept1, n21 = forward(1)
+    n21, up_far0, up_far1, n2_sent0, other_weights = fence(
+        n21, *up_far, n2_sent0, other_weights
+    )
+    weights = jnp.concatenate([own_weights, other_weights], axis=1)
+    attended = (kept0, kept1)
+
+    near0 = jnp.concatenate([n20, n2_sent0], axis=0)
+    n2_sent1 = swap(n21, across)
+    far0 = swap(near0, core)
+    sn0, bn0, grads = feed_forward(at_y, near0, up_near[0], weights)
+    sn0, bn0, grads, n2_sent1, far0 = fence(sn0, bn0, grads, n2_sent1, far0)
+    near1 = jnp.concatenate([n21, n2_sent1], axis=0)
+    far1 = swap(near1, core)
+    sf0, bf0, grads = feed_forward(at_y, after(far0, near1), up_far0, weights, grads)
+    sf0, bf0, grads, far1 = fence(sf0, bf0, grads, far1)
+    sf0_got = swap(sf0, core)
+    sn1, bn1, grads = feed_forward(at_y, near1, up_near[1], weights, grads)
+    sn1, bn1, grads, sf0_got = fence(sn1, bn1, grads, sf0_got)
+    sum0 = add(sn0, sf0_got)
+    theirs = sum0[local:]
+    across0 = swap(theirs, across)
+    sf1, bf1, grads = feed_forward(
+        at_y, after(far1, theirs), up_far1, weights, grads, True
+    )
+    sf1, bf1, grads, across0 = fence(sf1, bf1, grads, across0)
+    block_part = lax.psum_scatter(
+        grads.reshape(-1, width), ("y", "batch"), scatter_dimension=0, tiled=True
+    )
+
+    def residual_of(b, mine, got):
+        mixed, out_t, lse, hidden = attended[b]
+        return residual(
+            mine, got, ups[b], hidden, gain2, output_weight, out_t, (2, 3, 5, 6)
+        )
+
+    sf1_got = swap(sf1, core)
+    residual0 = residual_of(0, sum0[:local], across0)
+    *residual0, sf1_got = fence(*residual0, sf1_got)
+    sum1 = add(sn1, sf1_got)
+    theirs = sum1[local:]
+
+    def back(b, outs, *hold):
+        res, low, dot, delta, gain_share = outs
+        fac, qt, qmix, qbase, normed = projected[b]
+        return attend_backward(
+            (40, 0.1)[b], spans[b], qt, *gathered[b], info[b], after(dot, *hold), attended[b][2], delta,
+            qmix, qbase, cosine[b], sine[b],
+        )
+
+    across1 = swap(theirs, across)
+    bf_got = [swap(value, core) for value in (bf0, bf1)]
+    dnear0, dfar0, dq0 = back(0, residual0, theirs)
+    dnear0, dfar0, dq0, across1, *bf_got = fence(dnear0, dfar0, dq0, across1, *bf_got)
+    dfar0_got = swap(dfar0, core)
+    residual1 = residual_of(1, sum1[:local], across1)
+    *residual1, dnear0, dfar0_got = fence(*residual1, dnear0, dfar0_got)
+    residuals = (residual0, residual1)
+    fsum0 = add(dnear0, dfar0_got)
+    fparts0 = send_slots(fsum0)
+    wo_grad = sum(
+        mm_tn(after(attended[b][0], fsum0), residuals[b][1]) for b in range(rows)
+    ).astype(BF16)
+    slots = wo_grad.reshape(n, width // n, width)
+    order = [me ^ (2 * i) for i in range(n // 2)]
+    wo_near = jnp.stack([lax.dynamic_index_in_dim(slots, i, 0, keepdims=False) for i in order])
+    wo_far = jnp.stack([lax.dynamic_index_in_dim(slots, i ^ 1, 0, keepdims=False) for i in order])
+    wo_got = swap(wo_far, core)
+    dnear1, dfar1, dq1 = back(1, residual1, wo_far)
+    dnear1, dfar1, dq1, wo_got, *fparts0 = fence(dnear1, dfar1, dq1, wo_got, *fparts0)
+
+    dfar1_got = swap(dfar1, core)
+    branches = [
+        add(near, after(got, dnear1)) for near, got in zip((bn0, bn1), bf_got)
+    ]
+    branch_theirs = jnp.concatenate([value[local:] for value in branches], axis=0)
+    dfar1_got, dnear1, branch_theirs = fence(dfar1_got, dnear1, branch_theirs)
+    fsum1 = add(dnear1, dfar1_got)
+    fparts1 = send_slots(fsum1)
+    low0, grad0, gain_share0 = finish(
+        [fsum0[0], after(fparts0[0], fsum1)] + list(fparts0[1:]),
+        dq0, cosine[0], sine[0], xs[0], gain1, residual0[0], narrow,
+    )
+    wo_sum = add(wo_near, after(wo_got, low0))
+    *fparts1, fsum1, wo_sum, block_part = fence(*fparts1, fsum1, wo_sum, block_part)
+    block_grad = lax.all_gather(block_part, "batch", axis=0, tiled=True)
+    low1, grad1, gain_share1 = finish(
+        [fsum1[0]] + list(fparts1),
+        dq1, cosine[1], sine[1], xs[1], gain1, residual1[0], narrow,
+    )
+    near, far = share(
+        me.reshape(1),
+        (low0, low1),
+        [projected[b][4] for b in range(rows)],
+        (gain_share0, gain_share1),
+        (residual0[4], residual1[4]),
+        n,
+    )
+    far_got = swap(far, core)
+    wo_sent = send_slots(after(wo_sum, near))
+    far_got, near, wo_own = fence(far_got, near, wo_sum[0])
+    small = add(near, far_got)
+    small_sent = send_slots(after(small, *wo_sent))
+    wo_total = add(wo_own, *wo_sent)
+    wo_got = swap_batch(wo_total, 1)
+    branch_got = swap(after(branch_theirs, small), across)
+    *small_sent, small, wo_total, wo_got = fence(*small_sent, small, wo_total, wo_got)
+    small = add(small[0], *small_sent)
+    small_got = swap_batch(small, 1)
+    wo_total = add(wo_total, wo_got)
+    wo_got = swap_batch(wo_total, depth - 1)
+    tokens_gradient = jnp.stack([after(grad0, wo_total), grad1], axis=1)
+    tokens_gradient, small_got = fence(tokens_gradient, small_got)
+    small = add(small, small_got)
+    small_got = swap_batch(small, depth - 1)
+    outputs = []
+    for b in range(rows):
+        mine = branches[b][:local].astype(F32)
+        got = after(branch_got, small)[b * local : (b + 1) * local].astype(F32)
+        outputs.append(
+            jnp.where(valid[b][:, None], attended[b][3] + (mine + got), 0.0).astype(BF16)
+        )
+    output = jnp.stack(outputs, axis=1)
+    output_weight_grad = wo_total.astype(F32) + after(wo_got, output).astype(F32)
+    small = small.astype(F32) + after(small_got, output_weight_grad).astype(F32)
+    hid = gate_weight.shape[1]
+    block_grad = after(block_grad, small).astype(F32)
+    down_grad = block_grad[:hid]
+    gate_grad = block_grad[hid : 2 * hid].T
+    lift_grad = block_grad[2 * hid :].T
+    count = width // n
+
+    def pick(at, size):
+        return small[at : at + size].T
+
+    query_heads_grad = pick(0, QMIX)
+    query_basis_grad = pick(QMIX, QBASE)
+    at = QMIX + QBASE
+    key_heads_grad = pick(at, MIX)
+    key_basis_grad = pick(at + MIX, BASE)
+    value_heads_grad = pick(at + MIX + BASE, MIX)
+    value_basis_grad = pick(at + 2 * MIX + BASE, BASE)
+    at = at + FACTORS
+    first_gain_grad = small[at].reshape(count)
+    second_gain_grad = small[at + 1].reshape(count)
+
+    return (
+        output,
+        tokens_gradient,
+        first_gain_grad,
+        query_heads_grad,
+        query_basis_grad,
+        key_heads_grad,
+        key_basis_grad,
+        value_heads_grad,
+        value_basis_grad,
+        output_weight_grad,
+        second_gain_grad,
+        gate_grad,
+        lift_grad,
+        down_grad,
+    )
+
+
 def solution(mesh):
+    batch, wide = mesh.shape["batch"], mesh.shape["wide"]
+    split = wide == 8 and batch == 4
+    w = "wide"
+    if split:
+        mesh = jax.sharding.Mesh(
+            mesh.devices.reshape(batch, 2, 2, 2), ("batch", "y", "x", "core")
+        )
+        w = ("y", "x", "core")
+    rows = P(w, "batch", None)
     return jax.shard_map(
-        body,
+        body if split else general_body,
         mesh=mesh,
-        in_specs=(
-            P("wide", "batch", None),
-            P("batch", None),
-            P("wide", "batch", None),
-            P(),
-            P(),
-            P(),
-            P(),
-            P(),
-            P(),
-            P(),
-            P(),
-            P(),
-            P(None, "wide"),
-            P(None, "wide"),
-            P("wide", None),
-        ),
-        out_specs=(
-            P("wide", "batch", None),
-            P("wide", "batch", None),
-            P("wide"),
-            P("wide", None),
-            P("wide", None),
-            P("wide", None),
-            P("wide", None),
-            P("wide", None),
-            P("wide", None),
-            P("wide", None),
-            P("wide"),
-            P(None, "wide"),
-            P(None, "wide"),
-            P("wide", None),
-        ),
+        in_specs=(rows, P("batch", None), rows)
+        + (P(),) * 9
+        + (P(None, w), P(None, w), P(w, None)),
+        out_specs=(rows, rows, P(w))
+        + (P(w, None),) * 7
+        + (P(w), P(None, w), P(None, w), P(w, None)),
         check_vma=False,
     )

time: 1650 us -> 354 us (0.21)
  matrix products: 540 us -> 1.5 us
  waiting for transfers between devices: 597 us -> 105 us
  local copies, waits for them, and re-layouts: 319 us -> 39.4 us
  Pallas kernels: 0 us -> 95.7 us
  other arithmetic: 107 us -> 22.3 us
  starting transfers between devices: 1.71 us -> 71 us
  loops' own time: 41.3 us -> 0 us
    dot_general x75 -> x2, matrix products: 540 us -> 1.5 us  [mm_tn(): lax.dot_general(a, b, (((0,), (0,)), ((), ())), preferred_element_type=F32)]
    reduce_scatter x5 -> x1, waiting for transfers between devices: 285 us -> 4.76 us  [body(): lax.psum_scatter(grads.reshape(-1, width), ('y', 'batch'), scatter_dimens...]
    psum x2 -> x0, waiting for transfers between devices: 125 us -> none  [the longest x1 94.4 us: body(): lax.psum(qbasis_share.astype(jnp.bfloat16), 'batch').astype(jnp.float32)]
    ppermute x0 -> x43, waiting for transfers between devices: none -> 100 us  [the longest x39 70.2 us: swap(): return lax.ppermute(value, wide, partners(distance, n))]
    all_gather x3 -> x1, waiting for transfers between devices: 100 us -> 0.01 us  [body(): block_grad = lax.all_gather(block_part, 'batch', axis=0, tiled=True)]
    pallas_call x0 -> x15, Pallas kernels: none -> 95.7 us  [kernel_call(): pl.pallas_call(kernel, out_shape=tuple((pltpu.HBM(s, t) if i in kept else...]
    unnamed x20 -> x2, waiting for transfers between devices: 87.3 us -> 0.03 us
    ppermute x0 -> x43, starting transfers between devices: none -> 70.9 us  [the longest x39 48 us: swap(): return lax.ppermute(value, wide, partners(distance, n))]
  transfers between devices with their start and end apart: 15 -> 45, of which waited for: 13 -> 18; matrix products, arithmetic and copies ran while one was open for 10% -> 10% of each run, Pallas kernels for 0% -> 25%
where the time goes in v1:
time: 354 us; the launch traced here: 351 us
  waiting for transfers between devices  105 us (30%)
  Pallas kernels  95.7 us (27%)
  starting transfers between devices  71 us (20%)
  local copies, waits for them, and re-layouts  39.4 us (11%)
  other arithmetic  22.3 us (6%)
  between operations  15.7 us (4%)
    pallas_call x15, Pallas kernels, kernel_call(): pl.pallas_call(kernel, out_shape=tuple((pltpu.HBM(s, t) if i in kept else...  95.7 us
    ppermute x39, waiting for transfers between devices, swap(): return lax.ppermute(value, wide, partners(distance, n))  70.2 us
    ppermute x39, starting transfers between devices, swap(): return lax.ppermute(value, wide, partners(distance, n))  48 us
    ppermute x4, waiting for transfers between devices, swap_batch(): return lax.ppermute(value, 'batch', partners(distance, depth))  30 us
    unnamed x179, local copies, waits for them, and re-layouts  24.2 us
    ppermute x4, starting transfers between devices, swap_batch(): return lax.ppermute(value, 'batch', partners(distance, depth))  23 us
    convert_element_type x12, other arithmetic, add(): return sum((value.astype(F32) for value in values)).astype(BF16)  11.2 us
  transfers between devices with their start and end apart: 45, of which 18 were waited for; matrix products, arithmetic and copies ran while one was open for 10% of the time, Pallas kernels for 25%

profile of v1, /device:TPU:8, one launch (start us, length us, event | category | flops | bytes accessed | tf_op | source)
XLA Modules:
  0.0 350.7 jit_solution(2568881017516945043)
XLA Ops:
  8.3 3.4 fusion.11
  13.1 2.8 project.2
  19.5 2.8 project.3
  34.8 5.7 %attend_forward.2 = (bf16[256,1024]{1,0:T(8,128)(2,1)}, f32[1024,256]{1,0:T(8,128)}, f32[16,256]{1,0:T(8,128)}, f32[256,1024]{1,0:T(8,128)}, bf16[256,1024]{1,0:T(8,128)(2,1)S(1)}) custom-call(s32[3]{0:T(128)S(1)} %get-tuple-element.386.span, bf16[1024,256]{1,0:T(8,128)(2,1)S(1)} %copy-done.54, bf16[4,320,256]{2,1,0:T(8,128)(2,1)S(1)} %pad_maximum_fusion.9.near_ref, ...), custom_call_target="tpu_custom_call" | custom-call | flops 10000000000 | bytes 10000000 | tf_op jit(solution)/shard_map/attend_forward/pallas_call | solution.py:61
  40.6 17.3 %collective-permute-done.4 = bf16[512,1024]{1,0:T(8,128)(2,1)S(1)} collective-permute-done((bf16[512,1024]{1,0:T(8,128)(2,1)S(1)}, bf16[512,1024]{1,0:T(8,128)(2,1)S(1)}, u32[]{:S(2)}, u32[]{:S(2)}) %collective-permute-start.4) | collective-permute-done | bytes 1048608 | tf_op jit(solution)/shard_map/ppermute | solution.py:1116
  61.7 5.5 %attend_forward.3 = (bf16[256,1024]{1,0:T(8,128)(2,1)}, f32[1024,256]{1,0:T(8,128)}, f32[16,256]{1,0:T(8,128)}, f32[256,1024]{1,0:T(8,128)}, bf16[256,1024]{1,0:T(8,128)(2,1)S(1)}) custom-call(s32[3]{0:T(128)S(1)} %get-tuple-element.387.span, bf16[1024,256]{1,0:T(8,128)(2,1)S(1)} %copy-done.3, bf16[4,320,256]{2,1,0:T(8,128)(2,1)S(1)} %pad_maximum_fusion.10.near_ref, ...), custom_call_target="tpu_custom_call" | custom-call | flops 10000000000 | bytes 10000000 | tf_op jit(solution)/shard_map/attend_forward/pallas_call | solution.py:61
  67.3 6.1 %collective-permute-done.11 = bf16[256,1024]{1,0:T(8,128)(2,1)S(1)} collective-permute-done((bf16[256,1024]{1,0:T(8,128)(2,1)S(1)}, bf16[256,1024]{1,0:T(8,128)(2,1)S(1)}, u32[]{:S(2)}, u32[]{:S(2)}) %collective-permute-start.11) | collective-permute-done | bytes 524320 | tf_op jit(solution)/shard_map/ppermute | solution.py:1116
  73.4 9.6 %collective-permute-done.12 = bf16[3,352,1024]{2,1,0:T(8,128)(2,1)S(1)} collective-permute-done((bf16[3,352,1024]{2,1,0:T(8,128)(2,1)S(1)}, bf16[3,352,1024]{2,1,0:T(8,128)(2,1)S(1)}, u32[]{:S(2)}, u32[]{:S(2)}) %collective-permute-start.12) | collective-permute-done | bytes 2162720 | tf_op jit(solution)/shard_map/ppermute | solution.py:1116
  84.7 8.0 %feed_forward.4 = (bf16[512,1024]{1,0:T(8,128)(2,1)S(1)}, bf16[512,1024]{1,0:T(8,128)(2,1)}, f32[3,704,1024]{2,1,0:T(8,128)S(1)}) custom-call(s32[1]{0:T(128)} %bitcast.24.refs_0_, bf16[512,1024]{1,0:T(8,128)(2,1)S(1)} %constant_dynamic-update-slice_fusion.refs_1_, bf16[512,1024]{1,0:T(8,128)(2,1)S(1)} %pad_maximum_fusion.3.refs_2_, ...), custom_call_target="tpu_custom_call" | custom-call | flops 8999999488 | bytes 9000000 | tf_op jit(solution)/shard_map/feed_forward/pallas_call | solution.py:61
  92.8 5.8 %collective-permute-done.13 = bf16[256,1024]{1,0:T(8,128)(2,1)S(1)} collective-permute-done((bf16[256,1024]{1,0:T(8,128)(2,1)S(1)}, bf16[256,1024]{1,0:T(8,128)(2,1)S(1)}, u32[]{:S(2)}, u32[]{:S(2)}) %collective-permute-start.13) | collective-permute-done | bytes 524320 | tf_op jit(solution)/shard_map/ppermute | solution.py:1116
  98.6 9.2 %feed_forward.5 = (bf16[512,1024]{1,0:T(8,128)(2,1)S(1)}, bf16[512,1024]{1,0:T(8,128)(2,1)}, f32[3,704,1024]{2,1,0:T(8,128)S(1)}) custom-call(s32[1]{0:T(128)} %bitcast.24.refs_0_, bf16[512,1024]{1,0:T(8,128)(2,1)S(1)} %collective-permute-done.14.refs_1_, bf16[512,1024]{1,0:T(8,128)(2,1)S(1)} %collective-permute-done.9.refs_2_, ...), custom_call_target="tpu_custom_call", output_to_operand_aliasing={{2}: (4, {})} | custom-call | flops 8999999488 | bytes 9000000 | tf_op jit(solution)/shard_map/feed_forward/pallas_call | solution.py:61
  108.4 9.0 %feed_forward.6 = (bf16[512,1024]{1,0:T(8,128)(2,1)S(1)}, bf16[512,1024]{1,0:T(8,128)(2,1)}, f32[3,704,1024]{2,1,0:T(8,128)S(1)}) custom-call(s32[1]{0:T(128)} %bitcast.24.refs_0_, bf16[512,1024]{1,0:T(8,128)(2,1)S(1)} %constant_dynamic-update-slice_fusion.2.refs_1_, ...), custom_call_target="tpu_custom_call", output_to_operand_aliasing={{2}: (4, {})} | custom-call | flops 8999999488 | bytes 9000000 | tf_op jit(solution)/shard_map/feed_forward/pallas_call | solution.py:61
  118.4 10.9 %feed_forward.7 = (bf16[512,1024]{1,0:T(8,128)(2,1)}, bf16[512,1024]{1,0:T(8,128)(2,1)}, bf16[2,3,352,1024]{3,2,1,0:T(8,128)(2,1)}) custom-call(s32[1]{0:T(128)} %bitcast.24.refs_0_, bf16[512,1024]{1,0:T(8,128)(2,1)S(1)} %collective-permute-done.15.refs_1_, bf16[512,1024]{1,0:T(8,128)(2,1)S(1)} %collective-permute-done.10.refs_2_, ...), custom_call_target="tpu_custom_call" | custom-call | flops 8999999488 | bytes 9000000 | tf_op jit(solution)/shard_map/feed_forward/pallas_call | solution.py:61
  133.6 4.0 %residual.2 = (f32[256,1024]{1,0:T(8,128)}, bf16[256,1024]{1,0:T(8,128)(2,1)S(1)}, bf16[1024,256]{1,0:T(8,128)(2,1)S(1)}, f32[16,256]{1,0:T(8,128)S(1)}, f32[1,1024]{1,0:T(1,128)S(1)}) custom-call(bf16[256,1024]{1,0:T(8,128)(2,1)S(1)} %get-tuple-element.410.sa, bf16[256,1024]{1,0:T(8,128)(2,1)S(1)} %copy-done.24, bf16[256,1024]{1,0:T(8,128)(2,1)} %copy-done.59, ...), custom_call_target="tpu_custom_call" | custom-call | flops 3000000000 | bytes 3000000 | tf_op jit(solution)/shard_map/residual/pallas_call | solution.py:61
  140.7 12.5 %attend_backward.2 = (bf16[4,320,256]{2,1,0:T(8,128)(2,1)}, bf16[4,320,256]{2,1,0:T(8,128)(2,1)}, f32[480,256]{1,0:T(8,128)}) custom-call(s32[3]{0:T(128)} %copy-done.17, bf16[1024,256]{1,0:T(8,128)(2,1)} %get-tuple-element.172.qt_ref, bf16[4,320,256]{2,1,0:T(8,128)(2,1)} %copy-done.1, bf16[4,320,256]{2,1,0:T(8,128)(2,1)} %copy-done.22, ...), custom_call_target="tpu_custom_call" | custom-call | flops 40000000000 | bytes 40000000 | tf_op jit(solution)/shard_map/attend_backward/pallas_call | solution.py:61
  154.4 3.2 collective-permute-start.22
  157.6 4.3 %residual.3 = (f32[256,1024]{1,0:T(8,128)}, bf16[256,1024]{1,0:T(8,128)(2,1)S(1)}, bf16[1024,256]{1,0:T(8,128)(2,1)S(1)}, f32[16,256]{1,0:T(8,128)S(1)}, f32[1,1024]{1,0:T(1,128)S(1)}) custom-call(bf16[256,1024]{1,0:T(8,128)(2,1)S(1)} %get-tuple-element.407.sa, bf16[256,1024]{1,0:T(8,128)(2,1)S(1)} %collective-permute-done.19.sb, ...), custom_call_target="tpu_custom_call" | custom-call | flops 3000000000 | bytes 3000000 | tf_op jit(solution)/shard_map/residual/pallas_call | solution.py:61
  166.9 10.6 %collective-permute-start.24 = (bf16[320,256]{1,0:T(8,128)(2,1)S(1)}, bf16[320,256]{1,0:T(8,128)(2,1)S(1)}, u32[]{:S(2)}, u32[]{:S(2)}) collective-permute-start(bf16[320,256]{1,0:T(8,128)(2,1)S(1)} %get-tuple-element.426), channel_id=1, source_target_pairs={{0,2},{1,3},{2,0},{3,1},{4,6},{5,7},{6,4},{7,5},{8,10},{9,11},{10,... | collective-permute-start | bytes 491528 | tf_op jit(solution)/shard_map/ppermute | solution.py:1116
  179.0 15.2 %attend_backward.3 = (bf16[4,320,256]{2,1,0:T(8,128)(2,1)}, bf16[4,320,256]{2,1,0:T(8,128)(2,1)}, f32[480,256]{1,0:T(8,128)}) custom-call(s32[3]{0:T(128)} %copy-done.16, bf16[1024,256]{1,0:T(8,128)(2,1)} %get-tuple-element.185.qt_ref, bf16[4,320,256]{2,1,0:T(8,128)(2,1)} %copy-done, bf16[4,320,256]{2,1,0:T(8,128)(2,1)} %copy-done.2, s32[8,256]{1,0:T(8,128)} %copy-done.9, ...), custom_call_target="tpu_custom_call" | custom-call | flops 100000000 | bytes 100000 | tf_op jit(solution)/shard_map/attend_backward/pallas_call | solution.py:61
  206.3 6.1 %collective-permute-start.29 = (bf16[320,256]{1,0:T(8,128)(2,1)S(1)}, bf16[320,256]{1,0:T(8,128)(2,1)S(1)}, u32[]{:S(2)}, u32[]{:S(2)}) collective-permute-start(bf16[320,256]{1,0:T(8,128)(2,1)S(1)} %get-tuple-element.421), channel_id=1, source_target_pairs={{0,4},{1,5},{2,6},{3,7},{4,0},{5,1},{6,2},{7,3},{8,12},{9,13},{10,... | collective-permute-start | bytes 491528 | tf_op jit(solution)/shard_map/ppermute | solution.py:1116
  214.5 6.8 %collective-permute-done.29.refs_2_ = bf16[320,256]{1,0:T(8,128)(2,1)S(1)} collective-permute-done((bf16[320,256]{1,0:T(8,128)(2,1)S(1)}, bf16[320,256]{1,0:T(8,128)(2,1)S(1)}, u32[]{:S(2)}, u32[]{:S(2)}) %collective-permute-start.29) | collective-permute-done | bytes 163872 | tf_op jit(solution)/shard_map/ppermute | solution.py:1116
  222.6 4.8 %reduce-scatter.2.cloned.1.call-done = bf16[264,1024]{1,0:T(8,128)(2,1)} async-done(((bf16[2112,1024]{1,0:T(8,128)(2,1)}), bf16[264,1024]{1,0:T(8,128)(2,1)}) %reduce-scatter.2.cloned.1.call-update) | async-done | bytes 540688 | tf_op jit(solution)/shard_map/reduce_scatter | solution.py:1224
  246.5 4.8 %collective-permute-done.33 = bf16[128,1024]{1,0:T(8,128)(2,1)S(1)} collective-permute-done((bf16[128,1024]{1,0:T(8,128)(2,1)}, bf16[128,1024]{1,0:T(8,128)(2,1)S(1)}, u32[]{:S(2)}, u32[]{:S(2)}) %collective-permute-start.33) | collective-permute-done | bytes 262176 | tf_op jit(solution)/shard_map/ppermute | solution.py:1116
  251.3 6.4 %collective-permute-done.34 = bf16[128,1024]{1,0:T(8,128)(2,1)S(1)} collective-permute-done((bf16[128,1024]{1,0:T(8,128)(2,1)}, bf16[128,1024]{1,0:T(8,128)(2,1)S(1)}, u32[]{:S(2)}, u32[]{:S(2)}) %collective-permute-start.34) | collective-permute-done | bytes 262176 | tf_op jit(solution)/shard_map/ppermute | solution.py:1116
  258.9 20.3 %collective-permute-start.39 = (bf16[128,1024]{1,0:T(8,128)(2,1)S(1)}, bf16[128,1024]{1,0:T(8,128)(2,1)S(1)}, u32[]{:S(2)}, u32[]{:S(2)}) collective-permute-start(bf16[128,1024]{1,0:T(8,128)(2,1)S(1)} %add_convert_fusion.10), channel_id=1, source_target_pairs={{0,8},{8,0},{16,24},{24,16},{1,9},{9,1},{17,25},{25,17},{2,10},{10... | collective-permute-start | bytes 786440 | tf_op jit(solution)/shard_map/ppermute | solution.py:1119
  285.7 3.0 collective-permute-done.36
  291.4 3.0 collective-permute-done.38
  294.4 5.0 %collective-permute-done.39 = bf16[128,1024]{1,0:T(8,128)(2,1)S(1)} collective-permute-done((bf16[128,1024]{1,0:T(8,128)(2,1)S(1)}, bf16[128,1024]{1,0:T(8,128)(2,1)S(1)}, u32[]{:S(2)}, u32[]{:S(2)}) %collective-permute-start.39) | collective-permute-done | bytes 262176 | tf_op jit(solution)/shard_map/ppermute | solution.py:1119
  302.5 17.4 %collective-permute-done.40 = bf16[816,128]{1,0:T(8,128)(2,1)S(1)} collective-permute-done((bf16[816,128]{1,0:T(8,128)(2,1)S(1)}, bf16[816,128]{1,0:T(8,128)(2,1)S(1)}, u32[]{:S(2)}, u32[]{:S(2)}) %collective-permute-start.40) | collective-permute-done | bytes 208928 | tf_op jit(solution)/shard_map/ppermute | solution.py:1119
  320.0 2.9 copy.65
  325.5 4.1 %collective-permute-done.42 = bf16[128,1024]{1,0:T(8,128)(2,1)S(1)} collective-permute-done((bf16[128,1024]{1,0:T(8,128)(2,1)S(1)}, bf16[128,1024]{1,0:T(8,128)(2,1)S(1)}, u32[]{:S(2)}, u32[]{:S(2)}) %collective-permute-start.42) | collective-permute-done | bytes 262176 | tf_op jit(solution)/shard_map/ppermute | solution.py:1119
  330.5 3.5 %collective-permute-done.41 = bf16[816,128]{1,0:T(8,128)(2,1)S(1)} collective-permute-done((bf16[816,128]{1,0:T(8,128)(2,1)S(1)}, bf16[816,128]{1,0:T(8,128)(2,1)S(1)}, u32[]{:S(2)}, u32[]{:S(2)}) %collective-permute-start.41) | collective-permute-done | bytes 208928 | tf_op jit(solution)/shard_map/ppermute | solution.py:1119
  (332 shorter events, 101.0 us)
Async XLA Ops:
  7.2 220.2 %reduce-scatter.2.cloned.1.call-start = ((), (), s32[]{:S(2)}) async-start(), calls=%async_computation.1 | async-start | bytes 4866048 | tf_op jit(solution)/shard_map/reduce_scatter | solution.py:1224
  16.0 14.1 %collective-permute-start = (bf16[320,256]{1,0:T(8,128)(2,1)S(1)}, bf16[320,256]{1,0:T(8,128)(2,1)S(1)}, u32[]{:S(2)}, u32[]{:S(2)}) collective-permute-start(bf16[320,256]{1,0:T(8,128)(2,1)S(1)} %get-tuple-element.173), channel_id=1, source_target_pairs={{0,2},{1,3},{2,0},{3,1},{4,6},{5,7},{6,4},{7,5},{8,10},{9,11},{10,... | collective-permute-start | bytes 491528 | tf_op jit(solution)/shard_map/ppermute | solution.py:1116
  17.5 13.1 %collective-permute-start.1 = (bf16[320,256]{1,0:T(8,128)(2,1)S(1)}, bf16[320,256]{1,0:T(8,128)(2,1)S(1)}, u32[]{:S(2)}, u32[]{:S(2)}) collective-permute-start(bf16[320,256]{1,0:T(8,128)(2,1)S(1)} %get-tuple-element.173), channel_id=1, source_target_pairs={{0,4},{1,5},{2,6},{3,7},{4,0},{5,1},{6,2},{7,3},{8,12},{9,13},{10,... | collective-permute-start | bytes 491528 | tf_op jit(solution)/shard_map/ppermute | solution.py:1116
  19.0 11.6 %collective-permute-start.2 = (bf16[320,256]{1,0:T(8,128)(2,1)S(1)}, bf16[320,256]{1,0:T(8,128)(2,1)S(1)}, u32[]{:S(2)}, u32[]{:S(2)}) collective-permute-start(bf16[320,256]{1,0:T(8,128)(2,1)S(1)} %get-tuple-element.173), channel_id=1, source_target_pairs={{0,6},{1,7},{2,4},{3,5},{4,2},{5,3},{6,0},{7,1},{8,14},{9,15},{10,... | collective-permute-start | bytes 491528 | tf_op jit(solution)/shard_map/ppermute | solution.py:1116
  22.4 18.2 %collective-permute-start.5 = (bf16[320,256]{1,0:T(8,128)(2,1)S(1)}, bf16[320,256]{1,0:T(8,128)(2,1)S(1)}, u32[]{:S(2)}, u32[]{:S(2)}) collective-permute-start(bf16[320,256]{1,0:T(8,128)(2,1)S(1)} %get-tuple-element.175), channel_id=1, source_target_pairs={{0,2},{1,3},{2,0},{3,1},{4,6},{5,7},{6,4},{7,5},{8,10},{9,11},{10,... | collective-permute-start | bytes 491528 | tf_op jit(solution)/shard_map/ppermute | solution.py:1116
  23.8 16.7 %collective-permute-start.6 = (bf16[320,256]{1,0:T(8,128)(2,1)S(1)}, bf16[320,256]{1,0:T(8,128)(2,1)S(1)}, u32[]{:S(2)}, u32[]{:S(2)}) collective-permute-start(bf16[320,256]{1,0:T(8,128)(2,1)S(1)} %get-tuple-element.175), channel_id=1, source_target_pairs={{0,4},{1,5},{2,6},{3,7},{4,0},{5,1},{6,2},{7,3},{8,12},{9,13},{10,... | collective-permute-start | bytes 491528 | tf_op jit(solution)/shard_map/ppermute | solution.py:1116
  30.1 10.5 %collective-permute-start.7 = (bf16[320,256]{1,0:T(8,128)(2,1)S(1)}, bf16[320,256]{1,0:T(8,128)(2,1)S(1)}, u32[]{:S(2)}, u32[]{:S(2)}) collective-permute-start(bf16[320,256]{1,0:T(8,128)(2,1)S(1)} %get-tuple-element.175), channel_id=1, source_target_pairs={{0,6},{1,7},{2,4},{3,5},{4,2},{5,3},{6,0},{7,1},{8,14},{9,15},{10,... | collective-permute-start | bytes 491528 | tf_op jit(solution)/shard_map/ppermute | solution.py:1116
  31.6 26.3 %collective-permute-start.4 = (bf16[512,1024]{1,0:T(8,128)(2,1)S(1)}, bf16[512,1024]{1,0:T(8,128)(2,1)S(1)}, u32[]{:S(2)}, u32[]{:S(2)}) collective-permute-start(bf16[512,1024]{1,0:T(8,128)(2,1)S(1)} %pad_maximum_fusion.4), channel_id=1, source_target_pairs={{0,2},{1,3},{2,0},{3,1},{4,6},{5,7},{6,4},{7,5},{8,10},{9,11},{10,... | collective-permute-start | bytes 3145736 | tf_op jit(solution)/shard_map/ppermute | solution.py:1116
  33.2 49.8 %collective-permute-start.12 = (bf16[3,352,1024]{2,1,0:T(8,128)(2,1)S(1)}, bf16[3,352,1024]{2,1,0:T(8,128)(2,1)S(1)}, u32[]{:S(2)}, u32[]{:S(2)}) collective-permute-start(bf16[3,352,1024]{2,1,0:T(8,128)(2,1)S(1)} %pad_maximum_fusion.1), channel_id=1, source_target_pairs={{0,4},{1,5},{2,6},{3,7},{4,0},{5,1},{6,2},{7,3},{8,12},{9,13},{10,... | collective-permute-start | bytes 6488072 | tf_op jit(solution)/shard_map/ppermute | solution.py:1116
  59.0 14.3 %collective-permute-start.11 = (bf16[256,1024]{1,0:T(8,128)(2,1)S(1)}, bf16[256,1024]{1,0:T(8,128)(2,1)S(1)}, u32[]{:S(2)}, u32[]{:S(2)}) collective-permute-start(bf16[256,1024]{1,0:T(8,128)(2,1)S(1)} %get-tuple-element.184), channel_id=1, source_target_pairs={{0,2},{1,3},{2,0},{3,1},{4,6},{5,7},{6,4},{7,5},{8,10},{9,11},{10,... | collective-permute-start | bytes 1572872 | tf_op jit(solution)/shard_map/ppermute | solution.py:1116
  61.1 21.8 %collective-permute-start.10 = (bf16[512,1024]{1,0:T(8,128)(2,1)S(1)}, bf16[512,1024]{1,0:T(8,128)(2,1)S(1)}, u32[]{:S(2)}, u32[]{:S(2)}) collective-permute-start(bf16[512,1024]{1,0:T(8,128)(2,1)S(1)} %pad_maximum_fusion.5.refs_2_), channel_id=1, source_target_pairs={{0,1},{1,0},{2,3},{3,2},{4,5},{5,4},{6,7},{7,6},{8,9},{9,8},{10,11... | collective-permute-start | bytes 3145736 | tf_op jit(solution)/shard_map/ppermute | solution.py:1116
  61.3 21.7 %collective-permute-start.9 = (bf16[512,1024]{1,0:T(8,128)(2,1)S(1)}, bf16[512,1024]{1,0:T(8,128)(2,1)S(1)}, u32[]{:S(2)}, u32[]{:S(2)}) collective-permute-start(bf16[512,1024]{1,0:T(8,128)(2,1)S(1)} %pad_maximum_fusion.3.refs_2_), channel_id=1, source_target_pairs={{0,1},{1,0},{2,3},{3,2},{4,5},{5,4},{6,7},{7,6},{8,9},{9,8},{10,11... | collective-permute-start | bytes 3145736 | tf_op jit(solution)/shard_map/ppermute | solution.py:1116
  83.0 15.5 %collective-permute-start.14 = (bf16[512,1024]{1,0:T(8,128)(2,1)S(1)}, bf16[512,1024]{1,0:T(8,128)(2,1)S(1)}, u32[]{:S(2)}, u32[]{:S(2)}) collective-permute-start(bf16[512,1024]{1,0:T(8,128)(2,1)S(1)} %constant_dynamic-update-slice_fusion.refs_1_), channel_id=1, source_target_pairs={{0,1},{1,0},{2,3},{3,2},{4,5},{5,4},{6,7},{7,6},{8,9},{9,8},{10,11... | collective-permute-start | bytes 3145736 | tf_op jit(solution)/shard_map/ppermute | solution.py:1116
  84.2 14.4 %collective-permute-start.13 = (bf16[256,1024]{1,0:T(8,128)(2,1)S(1)}, bf16[256,1024]{1,0:T(8,128)(2,1)S(1)}, u32[]{:S(2)}, u32[]{:S(2)}) collective-permute-start(bf16[256,1024]{1,0:T(8,128)(2,1)S(1)} %get-tuple-element.200), channel_id=1, source_target_pairs={{0,2},{1,3},{2,0},{3,1},{4,6},{5,7},{6,4},{7,5},{8,10},{9,11},{10,... | collective-permute-start | bytes 1572872 | tf_op jit(solution)/shard_map/ppermute | solution.py:1116
  117.9 13.9 %collective-permute-start.17 = (bf16[256,1024]{1,0:T(8,128)(2,1)S(1)}, bf16[256,1024]{1,0:T(8,128)(2,1)S(1)}, u32[]{:S(2)}, u32[]{:S(2)}) collective-permute-start(bf16[256,1024]{1,0:T(8,128)(2,1)S(1)} %get-tuple-element.409), channel_id=1, source_target_pairs={{0,2},{1,3},{2,0},{3,1},{4,6},{5,7},{6,4},{7,5},{8,10},{9,11},{10,... | collective-permute-start | bytes 1572872 | tf_op jit(solution)/shard_map/ppermute | solution.py:1116
  131.8 21.5 %collective-permute-start.20 = (bf16[512,1024]{1,0:T(8,128)(2,1)}, bf16[512,1024]{1,0:T(8,128)(2,1)}, u32[]{:S(2)}, u32[]{:S(2)}) collective-permute-start(bf16[512,1024]{1,0:T(8,128)(2,1)} %get-tuple-element.243), channel_id=1, source_target_pairs={{0,1},{1,0},{2,3},{3,2},{4,5},{5,4},{6,7},{7,6},{8,9},{9,8},{10,11... | collective-permute-start | bytes 3145736 | tf_op jit(solution)/shard_map/ppermute | solution.py:1116
  132.3 21.0 %collective-permute-start.21 = (bf16[512,1024]{1,0:T(8,128)(2,1)}, bf16[512,1024]{1,0:T(8,128)(2,1)}, u32[]{:S(2)}, u32[]{:S(2)}) collective-permute-start(bf16[512,1024]{1,0:T(8,128)(2,1)} %get-tuple-element.244), channel_id=1, source_target_pairs={{0,1},{1,0},{2,3},{3,2},{4,5},{5,4},{6,7},{7,6},{8,9},{9,8},{10,11... | collective-permute-start | bytes 3145736 | tf_op jit(solution)/shard_map/ppermute | solution.py:1116
  132.6 205.6 %all-gather.2.cloned.1.call-start = ((), (), s32[]{:S(2)}) async-start(), calls=%async_computation.2 | async-start | bytes 2703360 | tf_op jit(solution)/shard_map/all_gather | solution.py:1283
  140.2 14.2 %collective-permute-start.19 = (bf16[256,1024]{1,0:T(8,128)(2,1)S(1)}, bf16[256,1024]{1,0:T(8,128)(2,1)S(1)}, u32[]{:S(2)}, u32[]{:S(2)}) collective-permute-start(bf16[256,1024]{1,0:T(8,128)(2,1)S(1)} %get-tuple-element.408), channel_id=1, source_target_pairs={{0,2},{1,3},{2,0},{3,1},{4,6},{5,7},{6,4},{7,5},{8,10},{9,11},{10,... | collective-permute-start | bytes 1572872 | tf_op jit(solution)/shard_map/ppermute | solution.py:1116
  166.7 27.5 %collective-permute-start.23 = (bf16[4,128,1024]{2,1,0:T(8,128)(2,1)S(1)}, bf16[4,128,1024]{2,1,0:T(8,128)(2,1)S(1)}, u32[]{:S(2)}, u32[]{:S(2)}) collective-permute-start(bf16[4,128,1024]{2,1,0:T(8,128)(2,1)S(1)} %pad_maximum_fusion.6), channel_id=1, source_target_pairs={{0,1},{1,0},{2,3},{3,2},{4,5},{5,4},{6,7},{7,6},{8,9},{9,8},{10,11... | collective-permute-start | bytes 3145736 | tf_op jit(solution)/shard_map/ppermute | solution.py:1116
  166.9 27.3 %collective-permute-start.24 = (bf16[320,256]{1,0:T(8,128)(2,1)S(1)}, bf16[320,256]{1,0:T(8,128)(2,1)S(1)}, u32[]{:S(2)}, u32[]{:S(2)}) collective-permute-start(bf16[320,256]{1,0:T(8,128)(2,1)S(1)} %get-tuple-element.426), channel_id=1, source_target_pairs={{0,2},{1,3},{2,0},{3,1},{4,6},{5,7},{6,4},{7,5},{8,10},{9,11},{10,... | collective-permute-start | bytes 491528 | tf_op jit(solution)/shard_map/ppermute | solution.py:1116
  177.5 16.8 %collective-permute-start.25 = (bf16[320,256]{1,0:T(8,128)(2,1)S(1)}, bf16[320,256]{1,0:T(8,128)(2,1)S(1)}, u32[]{:S(2)}, u32[]{:S(2)}) collective-permute-start(bf16[320,256]{1,0:T(8,128)(2,1)S(1)} %get-tuple-element.425), channel_id=1, source_target_pairs={{0,4},{1,5},{2,6},{3,7},{4,0},{5,1},{6,2},{7,3},{8,12},{9,13},{10,... | collective-permute-start | bytes 491528 | tf_op jit(solution)/shard_map/ppermute | solution.py:1116
  178.9 15.4 %collective-permute-start.26 = (bf16[320,256]{1,0:T(8,128)(2,1)S(1)}, bf16[320,256]{1,0:T(8,128)(2,1)S(1)}, u32[]{:S(2)}, u32[]{:S(2)}) collective-permute-start(bf16[320,256]{1,0:T(8,128)(2,1)S(1)} %get-tuple-element.424), channel_id=1, source_target_pairs={{0,6},{1,7},{2,4},{3,5},{4,2},{5,3},{6,0},{7,1},{8,14},{9,15},{10,... | collective-permute-start | bytes 491528 | tf_op jit(solution)/shard_map/ppermute | solution.py:1116
  206.3 14.9 %collective-permute-start.29 = (bf16[320,256]{1,0:T(8,128)(2,1)S(1)}, bf16[320,256]{1,0:T(8,128)(2,1)S(1)}, u32[]{:S(2)}, u32[]{:S(2)}) collective-permute-start(bf16[320,256]{1,0:T(8,128)(2,1)S(1)} %get-tuple-element.421), channel_id=1, source_target_pairs={{0,4},{1,5},{2,6},{3,7},{4,0},{5,1},{6,2},{7,3},{8,12},{9,13},{10,... | collective-permute-start | bytes 491528 | tf_op jit(solution)/shard_map/ppermute | solution.py:1116
  243.5 14.3 %collective-permute-start.34 = (bf16[128,1024]{1,0:T(8,128)(2,1)}, bf16[128,1024]{1,0:T(8,128)(2,1)S(1)}, u32[]{:S(2)}, u32[]{:S(2)}) collective-permute-start(bf16[128,1024]{1,0:T(8,128)(2,1)} %get-tuple-element.405), channel_id=1, source_target_pairs={{0,4},{1,5},{2,6},{3,7},{4,0},{5,1},{6,2},{7,3},{8,12},{9,13},{10,... | collective-permute-start | bytes 786440 | tf_op jit(solution)/shard_map/ppermute | solution.py:1116
  245.1 12.7 %collective-permute-start.35 = (bf16[128,1024]{1,0:T(8,128)(2,1)}, bf16[128,1024]{1,0:T(8,128)(2,1)}, u32[]{:S(2)}, u32[]{:S(2)}) collective-permute-start(bf16[128,1024]{1,0:T(8,128)(2,1)} %get-tuple-element.404), channel_id=1, source_target_pairs={{0,6},{1,7},{2,4},{3,5},{4,2},{5,3},{6,0},{7,1},{8,14},{9,15},{10,... | collective-permute-start | bytes 786440 | tf_op jit(solution)/shard_map/ppermute | solution.py:1116
  258.9 40.5 %collective-permute-start.39 = (bf16[128,1024]{1,0:T(8,128)(2,1)S(1)}, bf16[128,1024]{1,0:T(8,128)(2,1)S(1)}, u32[]{:S(2)}, u32[]{:S(2)}) collective-permute-start(bf16[128,1024]{1,0:T(8,128)(2,1)S(1)} %add_convert_fusion.10), channel_id=1, source_target_pairs={{0,8},{8,0},{16,24},{24,16},{1,9},{9,1},{17,25},{25,17},{2,10},{10... | collective-permute-start | bytes 786440 | tf_op jit(solution)/shard_map/ppermute | solution.py:1119
  282.7 11.7 %collective-permute-start.38 = (bf16[816,128]{1,0:T(8,128)(2,1)S(1)}, bf16[816,128]{1,0:T(8,128)(2,1)S(1)}, u32[]{:S(2)}, u32[]{:S(2)}) collective-permute-start(bf16[816,128]{1,0:T(8,128)(2,1)S(1)} %get-tuple-element.417), channel_id=1, source_target_pairs={{0,6},{1,7},{2,4},{3,5},{4,2},{5,3},{6,0},{7,1},{8,14},{9,15},{10,... | collective-permute-start | bytes 626696 | tf_op jit(solution)/shard_map/ppermute | solution.py:1116
  284.1 38.8 %collective-permute-start.32 = (bf16[512,1024]{1,0:T(8,128)(2,1)S(1)}, bf16[512,1024]{1,0:T(8,128)(2,1)S(1)}, u32[]{:S(2)}, u32[]{:S(2)}) collective-permute-start(bf16[512,1024]{1,0:T(8,128)(2,1)S(1)} %copy-done.76), channel_id=1, source_target_pairs={{0,2},{1,3},{2,0},{3,1},{4,6},{5,7},{6,4},{7,5},{8,10},{9,11},{10,... | collective-permute-start | bytes 3145736 | tf_op jit(solution)/shard_map/ppermute | solution.py:1116
  299.5 20.3 %collective-permute-start.40 = (bf16[816,128]{1,0:T(8,128)(2,1)S(1)}, bf16[816,128]{1,0:T(8,128)(2,1)S(1)}, u32[]{:S(2)}, u32[]{:S(2)}) collective-permute-start(bf16[816,128]{1,0:T(8,128)(2,1)S(1)} %fusion.6), channel_id=1, source_target_pairs={{0,8},{8,0},{16,24},{24,16},{1,9},{9,1},{17,25},{25,17},{2,10},{10... | collective-permute-start | bytes 626696 | tf_op jit(solution)/shard_map/ppermute | solution.py:1119
  302.1 27.5 %collective-permute-start.42 = (bf16[128,1024]{1,0:T(8,128)(2,1)S(1)}, bf16[128,1024]{1,0:T(8,128)(2,1)S(1)}, u32[]{:S(2)}, u32[]{:S(2)}) collective-permute-start(bf16[128,1024]{1,0:T(8,128)(2,1)S(1)} %add_convert_fusion.9), channel_id=1, source_target_pairs={{0,24},{8,16},{16,8},{24,0},{1,25},{9,17},{17,9},{25,1},{2,26},{10... | collective-permute-start | bytes 786440 | tf_op jit(solution)/shard_map/ppermute | solution.py:1119
  319.9 14.1 %collective-permute-start.41 = (bf16[816,128]{1,0:T(8,128)(2,1)S(1)}, bf16[816,128]{1,0:T(8,128)(2,1)S(1)}, u32[]{:S(2)}, u32[]{:S(2)}) collective-permute-start(bf16[816,128]{1,0:T(8,128)(2,1)S(1)} %add_convert_fusion.11), channel_id=1, source_target_pairs={{0,24},{8,16},{16,8},{24,0},{1,25},{9,17},{17,9},{25,1},{2,26},{10... | collective-permute-start | bytes 626696 | tf_op jit(solution)/shard_map/ppermute | solution.py:1119
  (99 other events, 679.7 us)
Sparse Core Ops, SparseCore 0:
  132.4 94.8 reduce-scatter.1
  245.6 78.6 all-gather.1
